TPU v7x, 128 devices: a whole 4x4x4 slice. The times are simulated.
128 devices in a mesh: grp: 2 (over x_hi), row: 8 (over z, x_lo), col: 8 (over y, core).
Axes of the slice: x: 4 (x_hi: 2, x_lo: 2; x = x_hi * 2 + x_lo), y: 4, z: 4, core: 2. Of those that a mesh axis runs over, the one named last changes fastest.
Arguments:
- alignment: bfloat16 [192, 1024, 256], P(('grp', 'row'), 'col'), may hold values from -10 to 10
- pair_features: bfloat16 [1024, 1024, 128], P(('grp', 'row'), 'col'), may hold values from -10 to 10
- w_bias: bfloat16 [128, 8], replicated, may hold values from -7.071068 to 7.071068
- query_weight: bfloat16 [256, 256], replicated, may hold values from -0.375 to 0.375
- key_value_weight: bfloat16 [256, 512], replicated, may hold values from -0.375 to 0.375
- gate_weight: bfloat16 [256, 256], replicated, may hold values from -0.375 to 0.375
- w_out: bfloat16 [256, 256], replicated, may hold values from -3 to 3
- w_left: bfloat16 [256, 32], replicated, may hold values from -0.375 to 0.375
- w_right: bfloat16 [256, 32], replicated, may hold values from -0.375 to 0.375
- w_outer: bfloat16 [1024, 128], replicated, may hold values from -1 to 1
Outputs:
- alignment_out: bfloat16 [192, 1024, 256], P(('grp', 'row'), 'col')
- pair_out: bfloat16 [1024, 1024, 128], P(('grp', 'row'), 'col')
All inputs are finite; a program needn't handle non-finite values.
Results may differ from a plain program's by a relative error of at most 0.009.
The roundings to bfloat16 on the way count: a program that leaves them out, or rounds other values in their place, can miss the bound.
Values may be sent and summed in bfloat16 or wider, within the bound.
A program may use at most 128 MiB of HBM per device.

v0:
```python
import math

import jax
import jax.numpy as jnp
from jax import lax
from jax.sharding import PartitionSpec as P

EPS = 1e-05


def layer_normalize(values_in):
    values_in = values_in.astype(jnp.float32)
    average = jnp.mean(values_in, axis=-1, keepdims=True)
    centered = values_in - average
    variance = jnp.mean(centered * centered, axis=-1, keepdims=True)
    return centered * lax.rsqrt(variance + EPS)


def shards(
    alignment,
    pair_features,
    w_bias,
    query_weight,
    key_value_weight,
    gate_weight,
    w_out,
    w_left,
    w_right,
    w_outer,
):
    residue_block = alignment.shape[1]
    alignment_width = alignment.shape[2]
    number_of_heads = w_bias.shape[1]
    per_head_width = alignment_width // number_of_heads
    pair_rows = pair_features.shape[0]
    pair_normed = layer_normalize(pair_features).astype(jnp.bfloat16)
    bias_tile = jnp.einsum(
        "ijc,ch->hij", pair_normed, w_bias, preferred_element_type=jnp.float32
    ).astype(jnp.bfloat16)
    bias_columns = lax.all_gather(bias_tile, ("grp", "row"), axis=1, tiled=True)
    bias_rows = lax.all_to_all(bias_columns, "col", split_axis=1, concat_axis=2, tiled=True)
    res_total = bias_rows.shape[2]
    alignment_normed_rows = layer_normalize(alignment).astype(jnp.bfloat16)
    query_rows = jnp.dot(
        alignment_normed_rows, query_weight, preferred_element_type=jnp.float32
    ).astype(jnp.bfloat16)
    gate_activation = jax.nn.sigmoid(
        jnp.dot(alignment_normed_rows, gate_weight, preferred_element_type=jnp.float32)
    )
    key_value_pair = jnp.dot(
        alignment_normed_rows, key_value_weight, preferred_element_type=jnp.float32
    ).astype(jnp.bfloat16)
    key_rows, value_rows = (
        lax.all_gather(key_value_pair[..., :alignment_width], "col", axis=1, tiled=True),
        lax.all_gather(key_value_pair[..., alignment_width:], "col", axis=1, tiled=True),
    )
    score_scale = 1.0 / math.sqrt(per_head_width)

    def attend(sequence_item):
        query_seq, key_seq, value_seq, gate_seq = sequence_item
        query_heads = query_seq.reshape(residue_block, number_of_heads, per_head_width)
        key_heads = key_seq.reshape(res_total, number_of_heads, per_head_width)
        value_heads = value_seq.reshape(res_total, number_of_heads, per_head_width)
        scores = jnp.einsum(
            "ihd,jhd->hij", query_heads, key_heads, preferred_element_type=jnp.float32
        ) * score_scale + bias_rows.astype(jnp.float32)
        row_max = jnp.max(scores, axis=-1, keepdims=True)
        exponent = jnp.exp(scores - row_max)
        weights = (exponent / jnp.sum(exponent, axis=-1, keepdims=True)).astype(jnp.bfloat16)
        attended = jnp.einsum(
            "hij,jhd->ihd", weights, value_heads, preferred_element_type=jnp.float32
        ).reshape(residue_block, alignment_width)
        return (gate_seq * attended).astype(jnp.bfloat16)

    attended_all = lax.map(attend, (query_rows, key_rows, value_rows, gate_activation))
    alignment_out = (
        alignment.astype(jnp.float32)
        + jnp.dot(attended_all, w_out, preferred_element_type=jnp.float32)
    ).astype(jnp.bfloat16)
    opm_normed = layer_normalize(alignment_out).astype(jnp.bfloat16)
    left_factor = jnp.einsum(
        "src,cd->sdr", opm_normed, w_left, preferred_element_type=jnp.float32
    ).astype(jnp.bfloat16)
    right_factor = jnp.einsum(
        "src,cd->sdr", opm_normed, w_right, preferred_element_type=jnp.float32
    ).astype(jnp.bfloat16)
    left_residues = lax.all_gather(left_factor, "col", axis=2, tiled=True)
    left_mine = lax.all_to_all(
        left_residues, ("grp", "row"), split_axis=2, concat_axis=0, tiled=True
    )
    right_sequences = lax.all_gather(right_factor, ("grp", "row"), axis=0, tiled=True)
    seq_count = left_mine.shape[0]
    opm_width = left_mine.shape[1]
    res_columns = right_sequences.shape[2]
    right_flat = right_sequences.reshape(seq_count, opm_width * res_columns)
    row_block = math.gcd(pair_rows, 8)
    left_blocks = left_mine.reshape(
        seq_count, opm_width, pair_rows // row_block, row_block
    ).transpose(2, 0, 1, 3)

    def outer_block(segment):
        flattened = segment.reshape(seq_count, opm_width * row_block)
        products = lax.dot_general(
            flattened, right_flat, (((0,), (0,)), ((), ())), preferred_element_type=jnp.float32
        )
        products = (
            (products / seq_count)
            .reshape(opm_width, row_block, opm_width, res_columns)
            .transpose(1, 3, 0, 2)
        )
        products = products.astype(jnp.bfloat16).reshape(
            row_block, res_columns, opm_width * opm_width
        )
        return jnp.dot(products, w_outer, preferred_element_type=jnp.float32)

    update = lax.map(outer_block, left_blocks).reshape(pair_rows, res_columns, w_outer.shape[1])
    pair_out = (pair_features.astype(jnp.float32) + update).astype(jnp.bfloat16)
    return (alignment_out, pair_out)


def solution(mesh):
    in_specs = (
        P(("grp", "row"), "col", None),
        P(("grp", "row"), "col", None),
        P(),
        P(),
        P(),
        P(),
        P(),
        P(),
        P(),
        P(),
    )
    out_specs = (P(("grp", "row"), "col", None), P(("grp", "row"), "col", None))
    return jax.shard_map(shards, mesh=mesh, in_specs=in_specs, out_specs=out_specs, check_vma=False)
```

profile of v0, /device:TPU:0, one launch (start us, length us, event | category | flops | bytes accessed | tf_op | source)
XLA Modules:
  0.0 446.3 jit_solution(12608857035141956544)
XLA Ops:
  12.0 3.5 fusion.45
  19.3 75.2 %all-gather.9.cloned.1.call-done = bf16[8,1024,128]{2,0,1:T(8,128)(2,1)} async-done(((bf16[8,64,128]{2,0,1:T(8,128)(2,1)}), bf16[8,1024,128]{2,0,1:T(8,128)(2,1)}) %all-gather.9.cloned.1.call-update) | async-done | bytes 2097168 | tf_op jit(solution)/shard_map/all_gather | solution.py:40
  94.5 4.3 all-to-all-start
  102.3 38.9 %all-to-all-done = bf16[8,1024,128]{2,0,1:T(8,128)(2,1)S(1)} async-done(((bf16[8,1024,128]{2,0,1:T(8,128)(2,1)}), bf16[8,1024,128]{2,0,1:T(8,128)(2,1)S(1)}, u32[]{:S(2)}, u32[]{:S(2)}) %all-to-all-start) | async-done | bytes 2097184 | tf_op jit(solution)/shard_map/all_to_all | solution.py:41
  143.9 4.2 all_to_all.27
  148.1 4.6 %all-gather.5.cloned.1.call-done = bf16[12,1024,256]{2,1,0:T(8,128)(2,1)} async-done(((bf16[12,128,256]{2,1,0:T(8,128)(2,1)}), bf16[12,1024,256]{2,1,0:T(8,128)(2,1)}) %all-gather.5.cloned.1.call-update) | async-done | bytes 6291472 | tf_op jit(solution)/shard_map/all_gather | solution.py:55
  152.7 41.7 %all-gather.7.cloned.1.call-done = bf16[12,1024,256]{2,1,0:T(8,128)(2,1)} async-done(((bf16[12,128,256]{2,1,0:T(8,128)(2,1)}), bf16[12,1024,256]{2,1,0:T(8,128)(2,1)}) %all-gather.7.cloned.1.call-update) | async-done | bytes 6291472 | tf_op jit(solution)/shard_map/all_gather | solution.py:54
  194.4 129.4 %while.20 = (s32[]{:T(128)}, bf16[12,128,256]{1,2,0:T(8,128)(2,1)}, f32[12,128,256]{2,1,0:T(8,128)}, bf16[12,1024,256]{2,1,0:T(8,128)(2,1)}, bf16[12,128,256]{2,...) while((s32[]{:T(128)}, bf16[12,128,256]{1,2,0:T(8,128)(2,1)}, ...), condition=%wide.region_7.8_spmd, body=%wide.region_4.7_spmd.sunk | while | flops 212929536 | bytes 11346529 | solution.py:75
  200.3 3.2 fusion.90
  211.0 3.2 fusion.90
  221.8 3.2 fusion.90
  232.6 3.2 fusion.90
  264.9 3.2 fusion.90
  297.3 3.2 fusion.90
  327.9 13.4 %all_gather.18 = bf16[12,32,1024]{2,1,0:T(8,128)(2,1)S(1)} all-gather(bf16[12,32,128]{2,1,0:T(8,128)(2,1)S(1)} %fusion.48), channel_id=1, replica_groups=mesh['grp'=2,'row'=8,'col'=8] {'col'}, dimensions={2}, use_global_device_ids=true | all-gather | bytes 884736 | tf_op jit(solution)/shard_map/all_gather | solution.py:87
  341.3 4.7 %copy.33 = bf16[12,32,1024]{1,0,2:T(8,128)(2,1)} copy(bf16[12,32,1024]{2,1,0:T(8,128)(2,1)S(1)} %all_gather.18) | data formatting | bytes 1572864 | tf_op jit(solution)/shard_map/all_gather | solution.py:87
  346.0 5.7 %reshape.88 = bf16[16,2,12288]{2,1,0:T(2,128)(2,1)} reshape(bf16[1024,12,32]{2,1,0:T(8,128)(2,1)} %bitcast.108) | data formatting | bytes 1572864
  351.8 6.9 %all-to-all-start.1 = ((bf16[16,2,12288]{2,1,0:T(2,128)(2,1)}), bf16[16,2,12288]{2,1,0:T(2,128)(2,1)S(1)}, u32[]{:S(2)}, u32[]{:S(2)}) async-start(bf16[16,2,12288]{2,1,0:T(2,128)(2,1)} %reshape.88), calls=%async_computation.1 | async-start | bytes 1572864 | tf_op jit(solution)/shard_map/all_to_all | solution.py:88
  358.7 20.8 %all-to-all-done.1 = bf16[16,2,12288]{2,1,0:T(2,128)(2,1)S(1)} async-done(((bf16[16,2,12288]{2,1,0:T(2,128)(2,1)}), bf16[16,2,12288]{2,1,0:T(2,128)(2,1)S(1)}, u32[]{:S(2)}, u32[]{:S(2)}) %all-to-all-start.1) | async-done | bytes 786464 | tf_op jit(solution)/shard_map/all_to_all | solution.py:88
  379.5 4.2 reshape.89
  386.7 4.0 copy.35
  390.7 16.5 %all-gather.11.cloned.1.call-done = bf16[192,32,128]{2,1,0:T(8,128)(2,1)} async-done(((bf16[12,32,128]{2,1,0:T(8,128)(2,1)}), bf16[192,32,128]{2,1,0:T(8,128)(2,1)}) %all-gather.11.cloned.1.call-update) | async-done | bytes 1572880 | tf_op jit(solution)/shard_map/all_gather | solution.py:91
  409.3 25.5 %while.21 = (s32[]{:T(128)}, f32[8,8,128,128]{3,2,1,0:T(8,128)}, bf16[8,192,32,8]{1,3,2,0:T(8,128)(2,1)}, bf16[192,4096]{1,0:T(8,128)(2,1)S(1)}, bf16[1024,128]{1,0:T(8,128)(2,1)S(1)}, /*index=5*/s32[]{:T(128)}) while((s32[]{:T(128)}, f32[8,8,128,128]{3,2,1,0:T(8,128)}, bf16[8,192,32,8]{1,3,2,0:T(8,128)(2,1)}, ...), condition=%wide.region_11.12_spmd, body=%wide.region_10.11_spmd.sunk | while | flops 673185792 | bytes 6685765 | solution.py:116
  434.8 5.0 %fusion.28 = bf16[64,128,128]{2,1,0:T(8,128)(2,1)} fusion(bf16[64,128,128]{2,1,0:T(8,128)(2,1)} %param.15, f32[8,8,128,128]{3,2,1,0:T(8,128)} %get-tuple-element.67), kind=kLoop, calls=%fused_computation.35 | loop fusion | flops 3145728 | bytes 8388608 | tf_op jit(solution)/shard_map/convert_element_type | solution.py:117
  (183 shorter events, 158.8 us)
Async XLA Ops:
  7.2 9.3 %copy-start = (bf16[256,512]{1,0:T(8,128)(2,1)S(1)}, bf16[256,512]{1,0:T(8,128)(2,1)}, u32[]{:S(2)}) copy-start(bf16[256,512]{1,0:T(8,128)(2,1)} %param.18) | copy-start | bytes 786436
  7.2 2.4 copy-start.1
  7.2 4.8 %copy-start.10 = (bf16[128,8]{0,1:T(8,128)(2,1)S(1)}, bf16[128,8]{0,1:T(8,128)(2,1)}, u32[]{:S(2)}) copy-start(bf16[128,8]{0,1:T(8,128)(2,1)} %param.16) | copy-start | bytes 6148
  7.2 87.3 %all-gather.9.cloned.1.call-start = ((), (), s32[]{:S(2)}) async-start(), calls=%async_computation.4 | async-start | bytes 2228224 | tf_op jit(solution)/shard_map/all_gather | solution.py:40
  12.0 3.7 copy-start.2
  15.6 137.1 %all-gather.5.cloned.1.call-start = ((), (), s32[]{:S(2)}) async-start(), calls=%async_computation.2 | async-start | bytes 7077888 | tf_op jit(solution)/shard_map/all_gather | solution.py:55
  18.5 175.8 %all-gather.7.cloned.1.call-start = ((), (), s32[]{:S(2)}) async-start(), calls=%async_computation.3 | async-start | bytes 7077888 | tf_op jit(solution)/shard_map/all_gather | solution.py:54
  19.3 79.7 %copy-start.6 = (bf16[256,256]{1,0:T(8,128)(2,1)S(1)}, bf16[256,256]{1,0:T(8,128)(2,1)}, u32[]{:S(2)}) copy-start(bf16[256,256]{1,0:T(8,128)(2,1)} %param.17) | copy-start | bytes 393220
  19.3 81.2 %copy-start.7 = (bf16[256,256]{1,0:T(8,128)(2,1)S(1)}, bf16[256,256]{1,0:T(8,128)(2,1)}, u32[]{:S(2)}) copy-start(bf16[256,256]{1,0:T(8,128)(2,1)} %param.19) | copy-start | bytes 393220
  94.5 46.8 %all-to-all-start = ((bf16[8,1024,128]{2,0,1:T(8,128)(2,1)}), bf16[8,1024,128]{2,0,1:T(8,128)(2,1)S(1)}, u32[]{:S(2)}, u32[]{:S(2)}) async-start(bf16[8,1024,128]{2,0,1:T(8,128)(2,1)} %all-gather.9.cloned.1.call-done), calls=%async_computation | async-start | bytes 4194304 | tf_op jit(solution)/shard_map/all_to_all | solution.py:41
  98.7 308.4 %all-gather.11.cloned.1.call-start = ((), (), s32[]{:S(2)}) async-start(), calls=%async_computation.5 | async-start | bytes 1671168 | tf_op jit(solution)/shard_map/all_gather | solution.py:91
  194.3 129.4 %copy-start.4 = (bf16[256,256]{1,0:T(8,128)(2,1)S(1)}, bf16[256,256]{1,0:T(8,128)(2,1)}, u32[]{:S(2)}) copy-start(bf16[256,256]{1,0:T(8,128)(2,1)} %param.20) | copy-start | bytes 393220
  323.7 2.2 copy-start.8
  323.7 3.5 copy-start.9
  325.4 15.9 %copy-start.3 = (bf16[12,128,256]{2,1,0:T(8,128)(2,1)}, bf16[12,128,256]{2,1,0:T(8,128)(2,1)S(1)}, u32[]{:S(2)}) copy-start(bf16[12,128,256]{2,1,0:T(8,128)(2,1)S(1)} %get-tuple-element.128) | copy-start | bytes 2359300
  351.8 27.7 %all-to-all-start.1 = ((bf16[16,2,12288]{2,1,0:T(2,128)(2,1)}), bf16[16,2,12288]{2,1,0:T(2,128)(2,1)S(1)}, u32[]{:S(2)}, u32[]{:S(2)}) async-start(bf16[16,2,12288]{2,1,0:T(2,128)(2,1)} %reshape.88), calls=%async_computation.1 | async-start | bytes 1572864 | tf_op jit(solution)/shard_map/all_to_all | solution.py:88
  390.7 18.6 %copy-start.5 = (bf16[1024,128]{1,0:T(8,128)(2,1)S(1)}, bf16[1024,128]{1,0:T(8,128)(2,1)}, u32[]{:S(2)}) copy-start(bf16[1024,128]{1,0:T(8,128)(2,1)} %param.23) | copy-start | bytes 786436
Sparse Core Ops, SparseCore 0:
  15.7 78.6 all-gather.8
  96.1 56.4 all-gather.4
  154.4 39.9 all-gather.6
  327.4 79.7 all-gather.10
where the time goes:
time: 449 us; the launch traced here: 446 us
  waiting for transfers between devices  198 us (44%)
  matrix products  114 us (25%)
  local copies, waits for them, and re-layouts  75.9 us (17%)
  other arithmetic  18.8 us (4%)
  between operations  14 us (3%)
  blocking collectives  13.4 us (3%)
  starting transfers between devices  11.6 us (3%)
    all_gather x1, waiting for transfers between devices, shards(): bias_columns = lax.all_gather(bias_tile, ('grp', 'row'), axis=1, tiled=True)  75.2 us
    dynamic_slice x84, local copies, waits for them, and re-layouts, shards(): lax.map(attend, (query_rows, key_rows, value_rows, gate_activation))  43.9 us
    all_gather x1, waiting for transfers between devices, shards(): lax.all_gather(key_value_pair[..., :alignment_width], 'col', axis=1, tile...  41.7 us
    all_to_all x1, waiting for transfers between devices, shards(): lax.all_to_all(bias_columns, 'col', split_axis=1, concat_axis=2, tiled=True)  38.9 us
    dot_general x12, matrix products, attend(): jnp.einsum('hij,jhd->ihd', weights, value_heads, preferred_element_type=j...  38.8 us
    sub x12, matrix products, attend(): exponent = jnp.exp(scores - row_max)  38.4 us
    all_to_all x1, waiting for transfers between devices, shards(): lax.all_to_all(left_residues, ('grp', 'row'), split_axis=2, concat_axis=0...  20.8 us
    all_gather x1, waiting for transfers between devices, shards(): lax.all_gather(right_factor, ('grp', 'row'), axis=0, tiled=True)  16.5 us
  transfers between devices with their start and end apart: 6, of which 6 were waited for; matrix products, arithmetic and copies ran while one was open for 7% of the time, Pallas kernels for 0%

commit v1 on v0

v1 whole, which is shorter than its diff:
```python
import functools
import math

import jax
import jax.numpy as jnp
from jax import lax
from jax.experimental import pallas as pl
from jax.experimental.pallas import tpu as pltpu
from jax.sharding import PartitionSpec as P

EPS = 1e-05
LOG2E = math.log2(math.e)
MESH = pl.DeviceIdType.MESH
F32, BF16 = jnp.float32, jnp.bfloat16
MIB = 1 << 20

RINGS = ({0: (1, 3), 1: (2,)}, {0: (1, 3), 3: (2,)})


def layer_normalize(values_in):
    values_in = values_in.astype(F32)
    average = jnp.mean(values_in, axis=-1, keepdims=True)
    centered = values_in - average
    variance = jnp.mean(centered * centered, axis=-1, keepdims=True)
    return centered * lax.rsqrt(variance + EPS)


class Place:
    def __init__(self):
        self.grp, self.row, self.col = (lax.axis_index(a) for a in ("grp", "row", "col"))
        self.x = 2 * self.grp + self.row % 2
        self.z = self.row // 2
        self.y = self.col // 2
        self.core = self.col % 2
        self.plane = 8 * self.grp + self.row

    def plane_index(self, dx, dz):
        x, z = (self.x + dx + 4) % 4, (self.z + dz + 4) % 4
        return 8 * (x // 2) + 2 * z + x % 2

    def in_plane(self, dx, dz):
        index = self.plane_index(dx, dz)
        return (index // 8, index % 8, self.col)

    def col_index(self, dy, dk):
        return 2 * ((self.y + dy + 4) % 4) + (self.core + dk) % 2

    def in_col(self, dy, dk):
        return (self.grp, self.row, self.col_index(dy, dk))


def plane_events():
    events = []
    for q in range(4):
        ring = RINGS[q % 2]
        level, depth = [(0, 0)], 0
        while level:
            following = []
            for first, second in level:
                kids = [(f, second) for f in ring.get(first, ())] if second == 0 else []
                kids += [(first, s) for s in ring.get(second, ())]
                turn = (lambda n: n) if q < 2 else (lambda n: (n[1], n[0]))
                events.append((depth, q, turn((first, second)), [turn(kid) for kid in kids]))
                following += kids
            level, depth = following, depth + 1
    return events


def col_events(pieces):
    events = []
    for q in range(pieces):
        ring = RINGS[q % 2]
        level, depth = [(0, 0)], 0
        while level:
            following = []
            for dy, dk in level:
                kids = [(d, 0) for d in ring.get(dy, ())] + [(dy, 1)] if dk == 0 else []
                events.append((depth, q, (dy, dk), kids))
                following += kids
            level, depth = following, depth + 1
    return events


class Spread:
    def __init__(self, target, source_of, slot, own, send_sem, recv_sem):
        self.target, self.source_of, self.slot, self.own = target, source_of, slot, own
        self.send_sem, self.recv_sem = send_sem, recv_sem
        self.started = []

    def run(self, event):
        _, q, node, kids = event
        source = self.source_of(-node[0], -node[1])
        here = self.slot(source, q)
        if node == (0, 0):
            origin = self.own(q)
        else:
            origin = here
            pltpu.make_async_remote_copy(
                src_ref=here,
                dst_ref=here,
                send_sem=self.send_sem.at[0],
                recv_sem=self.recv_sem.at[node[0] * 4 + node[1], q],
                device_id=self.target(0, 0),
                device_id_type=MESH,
            ).wait_recv()
        for kid in kids:
            step = ((kid[0] - node[0]) % 4, (kid[1] - node[1]) % 4)
            copy = pltpu.make_async_remote_copy(
                src_ref=origin,
                dst_ref=here,
                send_sem=self.send_sem.at[len(self.started)],
                recv_sem=self.recv_sem.at[kid[0] * 4 + kid[1], q],
                device_id=self.target(*step),
                device_id_type=MESH,
            )
            copy.start()
            self.started.append(copy)

    def finish(self):
        for copy in self.started:
            copy.wait_send()


def greet(place, partners, others):
    barrier = pltpu.get_barrier_semaphore()
    for partner in partners:
        pl.semaphore_signal(barrier, inc=1, device_id=partner, device_id_type=MESH)
    for other in others:
        pl.semaphore_signal(barrier, inc=1, device_id=other, device_id_type=MESH)
    return barrier, len(partners) + len(others)


def neighbours(place):
    return [place.in_plane(1, 0), place.in_plane(3, 0), place.in_plane(0, 1), place.in_plane(0, 3),
            place.in_col(1, 0), place.in_col(3, 0), place.in_col(0, 1)]


def scatter(copies, send_sem, recv_sem):
    started = []
    for n, (source, destination, device, is_self) in enumerate(copies):
        remote = pltpu.make_async_remote_copy(
            src_ref=source, dst_ref=destination, send_sem=send_sem.at[n], recv_sem=recv_sem, device_id=device, device_id_type=MESH
        )
        if is_self is None:
            remote.start()
        else:
            pl.when(jnp.logical_not(is_self))(remote.start)
            pl.when(is_self)(pltpu.make_async_copy(source, destination, recv_sem).start)
        started.append((remote, is_self))

    def finish():
        for remote, is_self in started:
            if is_self is None:
                remote.wait_send()
            else:
                pl.when(jnp.logical_not(is_self))(remote.wait_send)

    return finish


def prepare_kernel(
    pair_ref, msa_ref, wb_ref, x_all, bias_all, normed, tile32, tile,
    local_sem, scatter_send, scatter_recv, bias_send, bias_recv, x_send, x_recv,
):
    place = Place()
    barrier, expected = greet(
        place,
        neighbours(place),
        [((2 * place.col + u) // 8, (2 * place.col + u) % 8, c) for u in range(2) for c in range(8)],
    )

    seqs = msa_ref.shape[0]

    @pl.loop(0, seqs)
    def _(s):
        normed[s] = layer_normalize(msa_ref[s]).astype(BF16)

    pl.semaphore_wait(barrier, expected)

    part = seqs // 4
    x_spread = Spread(
        place.in_col,
        place.col_index,
        lambda source, q: x_all.at[source, pl.ds(q * part, part)],
        lambda q: normed.at[pl.ds(q * part, part)],
        x_send,
        x_recv,
    )
    x_todo = col_events(4)
    for event in [e for e in x_todo if e[0] == 0]:
        x_spread.run(event)
    keep = pltpu.make_async_copy(normed, x_all.at[place.col], local_sem)
    keep.start()

    weight = wb_ref[...].astype(F32).T.astype(BF16)
    rows = pair_ref.shape[0]
    heads = weight.shape[0]

    @pl.loop(0, rows, unroll=4)
    def _(i):
        pair_normed = layer_normalize(pair_ref[i]).astype(BF16)
        bias = lax.dot_general(weight, pair_normed, (((1,), (1,)), ((), ())), preferred_element_type=F32)
        tile32[pl.ds(i, heads, stride=rows), :] = bias

    tile[...] = tile32[...].astype(BF16).reshape(tile.shape)

    target_col = place.plane // 2
    copies = []
    for t in range(16):
        piece = (place.plane + t) % 16
        copies.append(
            (
                tile.at[piece],
                bias_all.at[piece, place.col, place.plane % 2],
                (piece // 8, piece % 8, target_col),
                target_col == place.col if t == 0 else None,
            )
        )
    scatter_finish = scatter(copies, scatter_send, scatter_recv)
    mine = bias_all.at[place.plane]
    pltpu.make_async_copy(mine, mine, scatter_recv).wait()

    bias_spread = Spread(
        place.in_plane,
        place.plane_index,
        lambda source, q: bias_all.at[source, pl.ds(2 * q, 2)],
        lambda q: bias_all.at[place.plane, pl.ds(2 * q, 2)],
        bias_send,
        bias_recv,
    )
    todo = [(3.0 * e[0], 0, bias_spread, e) for e in plane_events()]
    todo += [(6.0 * e[1] - 1 + 2 * (e[0] - 1), 1, x_spread, e) for e in x_todo if e[0] > 0]
    for _, _, spread, event in sorted(todo, key=lambda item: item[:2]):
        spread.run(event)
    keep.wait()
    scatter_finish()
    bias_spread.finish()
    x_spread.finish()


def attend_kernel(
    x_ref, msa_ref, bias_ref, wq_ref, wkv_ref, wg_ref, wo_ref, wl_ref, wr_ref,
    out_ref, left_ref, right_ref, bias_s, left_w, right_w, opm_s, left_s, right_s,
):
    step = pl.program_id(0)
    width = wq_ref.shape[0]
    heads = bias_s.shape[0]
    head_dim = width // heads
    opm = wl_ref.shape[1]
    group = 128 // opm
    dims_nt = (((1,), (1,)), ((), ()))

    @pl.when(step == 0)
    def _():
        for h in range(heads):
            for v in range(2):
                for u in range(2):
                    for c in range(8):
                        bias_s[h, u * 64 + v * 32 : u * 64 + v * 32 + 32, c * 128 : c * 128 + 128] = (
                            bias_ref[2 * h + v, c, u].astype(F32) * LOG2E
                        )
        left_s[...] = jnp.zeros_like(left_s)
        right_s[...] = jnp.zeros_like(right_s)
        spread_rows = lax.broadcasted_iota(jnp.int32, (opm, 128), 0)
        spread_lanes = lax.broadcasted_iota(jnp.int32, (opm, 128), 1)
        for b in range(group):
            place_b = (spread_lanes == spread_rows + b * opm).astype(F32).astype(BF16)
            left_w[b] = jnp.dot(wl_ref[...], place_b, preferred_element_type=F32).astype(BF16)
        eye = (
            lax.broadcasted_iota(jnp.int32, (opm, opm), 0) == lax.broadcasted_iota(jnp.int32, (opm, opm), 1)
        ).astype(F32).astype(BF16)
        right_w[...] = lax.dot_general(eye, wr_ref[...], dims_nt, preferred_element_type=F32).astype(BF16)

    col = lax.axis_index("col")
    own = x_ref[col, 0]
    everyone = x_ref[...].reshape(-1, width)
    queries = jnp.dot(own, wq_ref[...], preferred_element_type=F32).astype(BF16)
    gate = jax.nn.sigmoid(jnp.dot(own, wg_ref[...], preferred_element_type=F32))
    keys = jnp.dot(everyone, wkv_ref[:, :width], preferred_element_type=F32).astype(BF16)
    values = jnp.dot(everyone, wkv_ref[:, width:], preferred_element_type=F32).astype(BF16)
    head_of = lax.broadcasted_iota(jnp.int32, (own.shape[0], width), 1) // head_dim
    attended = jnp.zeros(own.shape, F32)
    zero = jnp.zeros_like(queries)
    for h in range(heads):
        query = jnp.where(head_of == h, queries, zero)
        scores = lax.dot_general(query, keys, dims_nt, preferred_element_type=F32)
        scores = scores * (LOG2E / math.sqrt(head_dim)) + bias_s[h]
        exponent = jnp.exp2(scores - jnp.max(scores, axis=-1, keepdims=True))
        inverse = 1.0 / jnp.sum(exponent, axis=-1, keepdims=True)
        weights = (exponent * inverse).astype(BF16)
        summed = jnp.dot(weights, values, preferred_element_type=F32)
        attended = jnp.where(head_of == h, summed, attended)
    attended = (gate * attended).astype(BF16)
    out = (msa_ref[0].astype(F32) + jnp.dot(attended, wo_ref[...], preferred_element_type=F32)).astype(BF16)
    out_ref[0] = out
    opm_normed = layer_normalize(out)
    for n in range(width // 128):
        opm_s[n] = opm_normed[:, n * 128 : n * 128 + 128]
    left = jnp.zeros((own.shape[0] // group, 128), F32)
    for b in range(group):
        for n in range(width // 128):
            some = opm_s[n, pl.ds(b, own.shape[0] // group, stride=group), :].astype(BF16)
            left += jnp.dot(some, left_w[b, n * 128 : n * 128 + 128], preferred_element_type=F32)
    rows = left.shape[0]
    left_s[pl.ds(step * rows, rows), :] = left
    right_s[pl.ds(step * opm, opm), :] = lax.dot_general(
        right_w[...], opm_normed.astype(BF16), dims_nt, preferred_element_type=F32
    )

    @pl.when(step == pl.num_programs(0) - 1)
    def _():
        for n in range(32):
            left_ref[n] = left_s[pl.ds(n, 16, stride=32), :].astype(BF16)
            right_ref[n] = right_s[pl.ds(n, 16, stride=32), :].astype(BF16)


def exchange_kernel(
    left_ref, right_ref, left_all, right_all, local_sem, scatter_send, scatter_recv, left_send, left_recv, right_send, right_recv
):
    place = Place()
    source_col = place.plane // 2
    barrier, expected = greet(place, neighbours(place), [(r // 8, r % 8, source_col) for r in range(16)])
    pl.semaphore_wait(barrier, expected)
    block = pl.ds(pl.multiple_of(place.plane * 16, 16), 16)

    def rows_of(source):
        return pl.ds(pl.multiple_of(source * 16, 16), 16)

    copies = []
    for half in range(2):
        row = 2 * place.col + half
        for t in range(8):
            c = (place.col + t) % 8
            copies.append(
                (
                    left_ref.at[pl.ds(16 * half + 2 * c, 2)],
                    left_all.at[pl.ds(2 * c, 2), block],
                    (row // 8, row % 8, c),
                    row == place.plane if t == 0 else None,
                )
            )
    scatter_finish = scatter(copies, scatter_send, scatter_recv)

    right_spread = Spread(
        place.in_plane,
        place.plane_index,
        lambda source, q: right_all.at[pl.ds(8 * q, 8), rows_of(source)],
        lambda q: right_ref.at[pl.ds(8 * q, 8)],
        right_send,
        right_recv,
    )
    plane = plane_events()
    for event in [e for e in plane if e[0] == 0]:
        right_spread.run(event)
    keep = pltpu.make_async_copy(right_ref, right_all.at[:, block], local_sem)
    keep.start()
    mine = left_all.at[pl.ds(2 * place.col, 2)]
    pltpu.make_async_copy(mine, mine, scatter_recv).wait()
    left_spread = Spread(
        place.in_col,
        place.col_index,
        lambda source, q: left_all.at[2 * source + q],
        lambda q: left_all.at[2 * place.col + q],
        left_send,
        left_recv,
    )
    todo = [(3.0 * e[0], 0, right_spread, e) for e in plane if e[0] > 0]
    todo += [(3.0 * e[0], 1, left_spread, e) for e in col_events(2)]
    for _, _, spread, event in sorted(todo, key=lambda item: item[:2]):
        spread.run(event)
    keep.wait()
    scatter_finish()
    left_spread.finish()
    right_spread.finish()


def outer_kernel(left_ref, right_ref, pair_ref, wo_ref, out_ref, w32, w_t, products, *, seqs):
    opm = right_ref.shape[0]
    group = 128 // opm

    @pl.when(pl.program_id(0) == 0)
    def _():
        w32[...] = wo_ref[...].astype(F32)
        turned = jnp.concatenate([w32[pl.ds(d, opm, stride=opm), :] for d in range(opm)], axis=0)
        w_t[...] = turned.T.astype(BF16)

    left = left_ref[0].T
    for d in range(0, opm, 2):
        right = jnp.concatenate([right_ref[d], right_ref[d + 1]], axis=1)
        product = (jnp.dot(left, right, preferred_element_type=F32) * (1.0 / seqs)).astype(BF16)
        for b in range(group):
            for e in range(2):
                products[b // 2, (d + e) * opm : (d + e + 1) * opm, (b % 2) * 128 : (b % 2) * 128 + 128] = product[
                    b * opm : (b + 1) * opm, e * 128 : e * 128 + 128
                ]
    for pair in range(group // 2):
        update = jnp.dot(w_t[...], products[pair], preferred_element_type=F32)
        for e in range(2):
            b = 2 * pair + e
            out_ref[b] = (pair_ref[b].astype(F32) + update[:, e * 128 : e * 128 + 128].T).astype(BF16)


def shards(
    alignment, pair_features, w_bias, query_weight, key_value_weight, gate_weight, w_out, w_left, w_right, w_outer
):
    seqs, residues, width = alignment.shape
    rows, columns, _ = pair_features.shape
    heads = w_bias.shape[1]
    opm = w_left.shape[1]
    anywhere = pl.BlockSpec(memory_space=pl.ANY)
    whole = pl.BlockSpec(memory_space=pltpu.VMEM)
    dma, regular = pltpu.SemaphoreType.DMA, pltpu.SemaphoreType.REGULAR
    x_all, bias_all = pl.pallas_call(
        prepare_kernel,
        out_shape=[
            jax.ShapeDtypeStruct((8, seqs, residues, width), BF16),
            jax.ShapeDtypeStruct((16, 8, 2, 32, 128), BF16),
        ],
        in_specs=[whole] * 3,
        out_specs=[anywhere] * 2,
        scratch_shapes=[
            pltpu.VMEM((seqs, residues, width), BF16),
            pltpu.VMEM((heads * rows, columns), F32),
            pltpu.VMEM((16, 32, columns), BF16),
            dma, dma((16,)), dma, dma((60,)), dma((16, 4)), dma((28,)), dma((16, 4)),
        ],
        compiler_params=pltpu.CompilerParams(collective_id=0, has_side_effects=True, vmem_limit_bytes=24 * MIB),
        name="prepare",
    )(pair_features, alignment, w_bias)

    def fixed(array):
        return pl.BlockSpec(array.shape, lambda s: (0,) * array.ndim)

    alignment_out, left, right = pl.pallas_call(
        attend_kernel,
        grid=(seqs,),
        out_shape=[
            jax.ShapeDtypeStruct(alignment.shape, BF16),
            jax.ShapeDtypeStruct((32, 16, 128), BF16),
            jax.ShapeDtypeStruct((32, 16, 128), BF16),
        ],
        in_specs=[
            pl.BlockSpec((8, 1, residues, width), lambda s: (0, s, 0, 0)),
            pl.BlockSpec((1, residues, width), lambda s: (s, 0, 0)),
            fixed(bias_all), fixed(query_weight), fixed(key_value_weight), fixed(gate_weight), fixed(w_out), fixed(w_left),
            fixed(w_right),
        ],
        out_specs=[
            pl.BlockSpec((1, residues, width), lambda s: (s, 0, 0)),
            pl.BlockSpec((32, 16, 128), lambda s: (0, 0, 0)),
            pl.BlockSpec((32, 16, 128), lambda s: (0, 0, 0)),
        ],
        scratch_shapes=[
            pltpu.VMEM((heads, residues, 8 * residues), F32),
            pltpu.VMEM((128 // opm, width, 128), BF16),
            pltpu.VMEM((opm, width), BF16),
            pltpu.VMEM((width // 128, residues, 128), F32),
            pltpu.VMEM((16 * 32, 128), F32),
            pltpu.VMEM((16 * 32, 128), F32),
        ],
        compiler_params=pltpu.CompilerParams(vmem_limit_bytes=48 * MIB),
        name="attend",
    )(x_all, alignment, bias_all, query_weight, key_value_weight, gate_weight, w_out, w_left, w_right)

    left_all, right_all = pl.pallas_call(
        exchange_kernel,
        out_shape=[
            jax.ShapeDtypeStruct((16, 256, 128), BF16),
            jax.ShapeDtypeStruct((32, 256, 128), BF16),
        ],
        in_specs=[whole] * 2,
        out_specs=[anywhere] * 2,
        scratch_shapes=[dma, dma((16,)), dma, dma((14,)), dma((16, 2)), dma((60,)), dma((16, 4))],
        compiler_params=pltpu.CompilerParams(collective_id=1, has_side_effects=True, vmem_limit_bytes=16 * MIB),
        name="exchange",
    )(left, right)

    pair_out = pl.pallas_call(
        functools.partial(outer_kernel, seqs=16 * seqs),
        grid=(rows * opm // 128,),
        out_shape=jax.ShapeDtypeStruct(pair_features.shape, BF16),
        in_specs=[
            pl.BlockSpec((1, 256, 128), lambda a: (a, 0, 0)),
            pl.BlockSpec((32, 256, 128), lambda a: (0, 0, 0)),
            pl.BlockSpec((128 // opm, columns, 128), lambda a: (a, 0, 0)),
            pl.BlockSpec(w_outer.shape, lambda a: (0, 0)),
        ],
        out_specs=pl.BlockSpec((128 // opm, columns, 128), lambda a: (a, 0, 0)),
        scratch_shapes=[
            pltpu.VMEM(w_outer.shape, F32),
            pltpu.VMEM(w_outer.shape[::-1], BF16),
            pltpu.VMEM((128 // opm // 2, w_outer.shape[0], 256), BF16),
        ],
        compiler_params=pltpu.CompilerParams(vmem_limit_bytes=32 * MIB),
        name="outer",
    )(left_all, right_all, pair_features, w_outer)
    return (alignment_out, pair_out)


def solution(mesh):
    rows = P(("grp", "row"), "col", None)
    in_specs = (rows, rows) + (P(),) * 8
    return jax.shard_map(shards, mesh=mesh, in_specs=in_specs, out_specs=(rows, rows), check_vma=False)
```

time: 449 us -> 177 us (0.39)
  waiting for transfers between devices: 198 us -> 0 us
  Pallas kernels: 0 us -> 168 us
  matrix products: 114 us -> 0 us
  local copies, waits for them, and re-layouts: 75.9 us -> 7.9 us
  other arithmetic: 18.8 us -> 0 us
  blocking collectives: 13.4 us -> 0 us
  between operations: 14 us -> 0.72 us
  starting transfers between devices: 11.6 us -> 0 us
    pallas_call x0 -> x4, Pallas kernels: none -> 168 us  [the longest x1 64.7 us: shards(): pl.pallas_call(attend_kernel, grid=(seqs,), out_shape=[jax.ShapeDtypeStru...]
    all_gather x4 -> x0, waiting for transfers between devices: 138 us -> none  [the longest x1 75.2 us: shards(): bias_columns = lax.all_gather(bias_tile, ('grp', 'row'), axis=1, tiled=True)]
    dot_general x35 -> x0, matrix products: 75.2 us -> none  [the longest x12 38.8 us: attend(): jnp.einsum('hij,jhd->ihd', weights, value_heads, preferred_element_type=j...]
    all_to_all x2 -> x0, waiting for transfers between devices: 59.7 us -> none  [the longest x1 38.9 us: shards(): lax.all_to_all(bias_columns, 'col', split_axis=1, concat_axis=2, tiled=True)]
    dynamic_slice x84 -> x0, local copies, waits for them, and re-layouts: 43.9 us -> none  [shards(): lax.map(attend, (query_rows, key_rows, value_rows, gate_activation))]
    sub x12 -> x0, matrix products: 38.4 us -> none  [attend(): exponent = jnp.exp(scores - row_max)]
    all_gather x1 -> x0, blocking collectives: 13.4 us -> none  [shards(): left_residues = lax.all_gather(left_factor, 'col', axis=2, tiled=True)]
    all_to_all x2 -> x0, starting transfers between devices: 11.2 us -> none  [the longest x1 6.95 us: shards(): lax.all_to_all(left_residues, ('grp', 'row'), split_axis=2, concat_axis=0...]
  transfers between devices with their start and end apart: 6 -> 0, of which waited for: 6 -> 0; matrix products, arithmetic and copies ran while one was open for 7% -> 0% of each run, Pallas kernels for 0% -> 0%
where the time goes in v1:
time: 177 us
  Pallas kernels  168 us (95%)
  local copies, waits for them, and re-layouts  7.9 us (4%)
    pallas_call x1, Pallas kernels, shards(): pl.pallas_call(attend_kernel, grid=(seqs,), out_shape=[jax.ShapeDtypeStru...  64.7 us
    pallas_call x1, Pallas kernels, shards(): pl.pallas_call(prepare_kernel, out_shape=[jax.ShapeDtypeStruct((8, seqs,...  61.7 us
    pallas_call x1, Pallas kernels, shards(): pl.pallas_call(exchange_kernel, out_shape=[jax.ShapeDtypeStruct((16, 256,...  28.7 us
    pallas_call x1, Pallas kernels, shards(): pl.pallas_call(functools.partial(outer_kernel, seqs=16 * seqs), grid=(row...  13.5 us
    unnamed x23, local copies, waits for them, and re-layouts  7.9 us

profile of v1, /device:TPU:0, one launch (start us, length us, event | category | flops | bytes accessed | tf_op | source)
XLA Modules:
  0.0 177.1 jit_solution(10360456084031780091)
XLA Ops:
  0.6 0.0 copy-start.7
  0.6 0.8 copy.12.wb_ref
  1.5 0.8 copy.13.wl_ref
  2.3 0.8 copy.14.wr_ref
  3.1 0.0 copy-start
  3.2 1.6 copy-done
  4.7 0.0 copy-start.3
  4.7 1.1 copy-done.3
  5.9 0.0 copy-start.4
  5.9 61.7 %prepare.1 = (bf16[8,12,128,256]{3,2,1,0:T(8,128)(2,1)S(1)}, bf16[16,8,2,32,128]{4,3,2,1,0:T(8,128)(2,1)S(1)}) custom-call(bf16[64,128,128]{2,1,0:T(8,128)(2,1)S(1)} %copy-done, bf16[12,128,256]{2,1,0:T(8,128)(2,1)S(1)} %copy-done.3, bf16[128,8]{1,0:T(8,128)(2,1)S(1)} %copy.12.wb_ref), custom_call_target="tpu_custom_call" | custom-call | tf_op jit(solution)/shard_map/prepare/pallas_call | solution.py:413
  67.6 0.0 copy-start.2
  67.6 2.6 %copy-done.2 = bf16[8,12,128,256]{3,2,1,0:T(8,128)(2,1)} copy-done((bf16[8,12,128,256]{3,2,1,0:T(8,128)(2,1)}, bf16[8,12,128,256]{3,2,1,0:T(8,128)(2,1)S(1)}, u32[]{:S(2)}) %copy-start.2) | copy-done | bytes 6291480
  70.3 0.0 copy-done.7
  70.3 0.0 copy-done.4
  70.3 0.0 copy-done.5
  70.3 0.0 copy-done.8
  70.3 0.0 copy-done.9
  70.3 0.0 copy-start.1
  70.3 0.0 copy-start.6
  70.3 64.7 %attend.1 = (bf16[12,128,256]{2,1,0:T(8,128)(2,1)}, bf16[32,16,128]{2,1,0:T(8,128)(2,1)S(1)}, bf16[32,16,128]{2,1,0:T(8,128)(2,1)S(1)}) custom-call(bf16[8,12,128,256]{3,2,1,0:T(8,128)(2,1)} %copy-done.2, bf16[12,128,256]{2,1,0:T(8,128)(2,1)S(1)} %copy-done.4, bf16[16,8,2,32,128]{4,3,2,1,0:T(8,128)(2,1)S(1)} %get-tuple-element.10.bias_ref, ...), custom_call_target="tpu_custom_call" | custom-call | tf_op jit(solution)/shard_map/attend/pallas_call | solution.py:434
  135.0 28.7 %exchange.1 = (bf16[16,256,128]{2,1,0:T(8,128)(2,1)S(1)}, bf16[32,256,128]{2,1,0:T(8,128)(2,1)S(1)}) custom-call(bf16[32,16,128]{2,1,0:T(8,128)(2,1)S(1)} %get-tuple-element.12.left_ref, bf16[32,16,128]{2,1,0:T(8,128)(2,1)S(1)} %get-tuple-element.13.right_ref), custom_call_target="tpu_custom_call" | custom-call | tf_op jit(solution)/shard_map/exchange/pallas_call | solution.py:465
  163.6 0.0 copy-done.1
  163.6 0.0 copy-done.6
  163.7 13.5 %outer.1 = bf16[64,128,128]{2,1,0:T(8,128)(2,1)} custom-call(bf16[16,256,128]{2,1,0:T(8,128)(2,1)S(1)} %get-tuple-element.14.left_ref, bf16[32,256,128]{2,1,0:T(8,128)(2,1)S(1)} %get-tuple-element.15.right_ref, bf16[64,128,128]{2,1,0:T(8,128)(2,1)S(1)} %copy-done.1, bf16[1024,128]{1,0:T(8,128)(2,1)S(1)} %copy-done.6), custom_call_target="tpu_custom_call" | custom-call | tf_op jit(solution)/shard_map/outer/pallas_call | solution.py:478
  (3 shorter events, 0.0 us)
Async XLA Ops:
  0.6 69.6 %copy-start.7 = (bf16[256,256]{1,0:T(8,128)(2,1)S(1)}, bf16[256,256]{1,0:T(8,128)(2,1)}, u32[]{:S(2)}) copy-start(bf16[256,256]{1,0:T(8,128)(2,1)} %wq_ref.1) | copy-start | bytes 393220
  3.1 1.6 copy-start
  4.7 1.1 copy-start.3
  5.9 64.4 %copy-start.4 = (bf16[12,128,256]{2,1,0:T(8,128)(2,1)S(1)}, bf16[12,128,256]{2,1,0:T(8,128)(2,1)}, u32[]{:S(2)}) copy-start(bf16[12,128,256]{2,1,0:T(8,128)(2,1)} %msa_ref.3) | copy-start | bytes 2359300
  5.9 64.4 %copy-start.5 = (bf16[256,512]{1,0:T(8,128)(2,1)S(1)}, bf16[256,512]{1,0:T(8,128)(2,1)}, u32[]{:S(2)}) copy-start(bf16[256,512]{1,0:T(8,128)(2,1)} %wkv_ref.1) | copy-start | bytes 786436
  5.9 64.4 %copy-start.8 = (bf16[256,256]{1,0:T(8,128)(2,1)S(1)}, bf16[256,256]{1,0:T(8,128)(2,1)}, u32[]{:S(2)}) copy-start(bf16[256,256]{1,0:T(8,128)(2,1)} %wg_ref.1) | copy-start | bytes 393220
  5.9 64.4 %copy-start.9 = (bf16[256,256]{1,0:T(8,128)(2,1)S(1)}, bf16[256,256]{1,0:T(8,128)(2,1)}, u32[]{:S(2)}) copy-start(bf16[256,256]{1,0:T(8,128)(2,1)} %wo_ref.2) | copy-start | bytes 393220
  67.6 2.7 %copy-start.2 = (bf16[8,12,128,256]{3,2,1,0:T(8,128)(2,1)}, bf16[8,12,128,256]{3,2,1,0:T(8,128)(2,1)S(1)}, u32[]{:S(2)}) copy-start(bf16[8,12,128,256]{3,2,1,0:T(8,128)(2,1)S(1)} %get-tuple-element.9.x_ref) | copy-start | bytes 18874372
  70.3 93.4 %copy-start.1 = (bf16[64,128,128]{2,1,0:T(8,128)(2,1)S(1)}, bf16[64,128,128]{2,1,0:T(8,128)(2,1)}, u32[]{:S(2)}) copy-start(bf16[64,128,128]{2,1,0:T(8,128)(2,1)} %pair_ref.3) | copy-start | bytes 6291460
  70.3 93.4 %copy-start.6 = (bf16[1024,128]{1,0:T(8,128)(2,1)S(1)}, bf16[1024,128]{1,0:T(8,128)(2,1)}, u32[]{:S(2)}) copy-start(bf16[1024,128]{1,0:T(8,128)(2,1)} %wo_ref.3) | copy-start | bytes 786436

commit v2 on v1

--- a/solution.py
+++ b/solution.py
@@ -159,9 +159,13 @@
 
 
 def prepare_kernel(
-    pair_ref, msa_ref, wb_ref, x_all, bias_all, normed, tile32, tile,
-    local_sem, scatter_send, scatter_recv, bias_send, bias_recv, x_send, x_recv,
+    pair_hbm, msa_hbm, wb_ref, x_all, bias_all, msa_ref, pair_ref, normed, tile32, tile,
+    in_sem, local_sem, scatter_send, scatter_recv, bias_send, bias_recv, x_send, x_recv,
 ):
+    get_msa = pltpu.make_async_copy(msa_hbm, msa_ref, in_sem.at[0])
+    get_msa.start()
+    get_pair = pltpu.make_async_copy(pair_hbm, pair_ref, in_sem.at[1])
+    get_pair.start()
     place = Place()
     barrier, expected = greet(
         place,
@@ -170,14 +174,8 @@
     )
 
     seqs = msa_ref.shape[0]
-
-    @pl.loop(0, seqs)
-    def _(s):
-        normed[s] = layer_normalize(msa_ref[s]).astype(BF16)
-
-    pl.semaphore_wait(barrier, expected)
-
-    part = seqs // 4
+    pieces, early = 6, 2
+    part = seqs // pieces
     x_spread = Spread(
         place.in_col,
         place.col_index,
@@ -186,20 +184,28 @@
         x_send,
         x_recv,
     )
-    x_todo = col_events(4)
-    for event in [e for e in x_todo if e[0] == 0]:
+    x_todo = col_events(pieces)
+    x_roots = [e for e in x_todo if e[0] == 0]
+    get_msa.wait()
+
+    @pl.loop(0, seqs)
+    def _(s):
+        normed[s] = layer_normalize(msa_ref[s]).astype(BF16)
+
+    pl.semaphore_wait(barrier, expected)
+    for event in x_roots[:early]:
         x_spread.run(event)
     keep = pltpu.make_async_copy(normed, x_all.at[place.col], local_sem)
     keep.start()
 
-    weight = wb_ref[...].astype(F32).T.astype(BF16)
     rows = pair_ref.shape[0]
-    heads = weight.shape[0]
-
-    @pl.loop(0, rows, unroll=4)
+    heads = wb_ref.shape[0]
+    get_pair.wait()
+
+    @pl.loop(0, rows, unroll=8)
     def _(i):
         pair_normed = layer_normalize(pair_ref[i]).astype(BF16)
-        bias = lax.dot_general(weight, pair_normed, (((1,), (1,)), ((), ())), preferred_element_type=F32)
+        bias = lax.dot_general(wb_ref[...], pair_normed, (((1,), (1,)), ((), ())), preferred_element_type=F32)
         tile32[pl.ds(i, heads, stride=rows), :] = bias
 
     tile[...] = tile32[...].astype(BF16).reshape(tile.shape)
@@ -217,9 +223,9 @@
             )
         )
     scatter_finish = scatter(copies, scatter_send, scatter_recv)
+    for event in x_roots[early:]:
+        x_spread.run(event)
     mine = bias_all.at[place.plane]
-    pltpu.make_async_copy(mine, mine, scatter_recv).wait()
-
     bias_spread = Spread(
         place.in_plane,
         place.plane_index,
@@ -228,9 +234,13 @@
         bias_send,
         bias_recv,
     )
-    todo = [(3.0 * e[0], 0, bias_spread, e) for e in plane_events()]
-    todo += [(6.0 * e[1] - 1 + 2 * (e[0] - 1), 1, x_spread, e) for e in x_todo if e[0] > 0]
-    for _, _, spread, event in sorted(todo, key=lambda item: item[:2]):
+    todo = [(14 + 4.5 * e[0], 0, e[1], bias_spread, e) for e in plane_events()]
+    todo += [(5 + 4 * e[1] if e[0] == 1 else 28 + e[0] + e[1], 1, e[1], x_spread, e) for e in x_todo if e[0] > 0]
+    scattered = False
+    for _, kind, _, spread, event in sorted(todo, key=lambda item: item[:3]):
+        if kind == 0 and not scattered:
+            pltpu.make_async_copy(mine, mine, scatter_recv).wait()
+            scattered = True
         spread.run(event)
     keep.wait()
     scatter_finish()
@@ -238,74 +248,129 @@
     x_spread.finish()
 
 
+def nt_dot(a, b):
+    return lax.dot_general(a, b, (((1,), (1,)), ((), ())), preferred_element_type=F32)
+
+
+def tn_dot(a, b):
+    return lax.dot_general(a, b, (((0,), (0,)), ((), ())), preferred_element_type=F32)
+
+
+def dot(a, b):
+    return jnp.dot(a, b, preferred_element_type=F32)
+
+
+def unit(rows, columns, shift=0):
+    row = lax.broadcasted_iota(jnp.int32, (rows, columns), 0)
+    column = lax.broadcasted_iota(jnp.int32, (rows, columns), 1)
+    return (column == row + shift).astype(F32).astype(BF16)
+
+
 def attend_kernel(
     x_ref, msa_ref, bias_ref, wq_ref, wkv_ref, wg_ref, wo_ref, wl_ref, wr_ref,
-    out_ref, left_ref, right_ref, bias_s, left_w, right_w, opm_s, left_s, right_s,
+    out_ref, left_ref, right_ref,
+    bias_s, left_w, opm_s, left_s, right_s, wt_s, k_s, vt_s, q_s, t_s, w_s, att_s, gate_s,
 ):
     step = pl.program_id(0)
-    width = wq_ref.shape[0]
-    heads = bias_s.shape[0]
+    seqs, queries, width = msa_ref.shape
+    keys = k_s.shape[1]
+    opm = wl_ref.shape[0]
+    group = 128 // opm
+    heads = 2 * bias_s.shape[0]
     head_dim = width // heads
-    opm = wl_ref.shape[1]
-    group = 128 // opm
-    dims_nt = (((1,), (1,)), ((), ()))
+    both = 2 * queries
+    chunk = 256
 
     @pl.when(step == 0)
     def _():
+        turn = unit(128, 128)
         for h in range(heads):
-            for v in range(2):
-                for u in range(2):
-                    for c in range(8):
-                        bias_s[h, u * 64 + v * 32 : u * 64 + v * 32 + 32, c * 128 : c * 128 + 128] = (
-                            bias_ref[2 * h + v, c, u].astype(F32) * LOG2E
-                        )
+            for c in range(8):
+                block = jnp.concatenate([bias_ref[2 * h + v, c, u] for u in range(2) for v in range(2)], axis=0)
+                bias_s[h // 2, c * 128 : c * 128 + 128, (h % 2) * 128 : (h % 2) * 128 + 128] = nt_dot(turn, block) * LOG2E
         left_s[...] = jnp.zeros_like(left_s)
         right_s[...] = jnp.zeros_like(right_s)
-        spread_rows = lax.broadcasted_iota(jnp.int32, (opm, 128), 0)
-        spread_lanes = lax.broadcasted_iota(jnp.int32, (opm, 128), 1)
         for b in range(group):
-            place_b = (spread_lanes == spread_rows + b * opm).astype(F32).astype(BF16)
-            left_w[b] = jnp.dot(wl_ref[...], place_b, preferred_element_type=F32).astype(BF16)
-        eye = (
-            lax.broadcasted_iota(jnp.int32, (opm, opm), 0) == lax.broadcasted_iota(jnp.int32, (opm, opm), 1)
-        ).astype(F32).astype(BF16)
-        right_w[...] = lax.dot_general(eye, wr_ref[...], dims_nt, preferred_element_type=F32).astype(BF16)
+            left_w[b] = tn_dot(wl_ref[...], unit(opm, 128, b * opm)).astype(BF16)
+        wt_s[0] = wq_ref[...].T
+        wt_s[1] = wkv_ref[:, width:].T
+        wt_s[2] = wg_ref[...].T
 
     col = lax.axis_index("col")
-    own = x_ref[col, 0]
-    everyone = x_ref[...].reshape(-1, width)
-    queries = jnp.dot(own, wq_ref[...], preferred_element_type=F32).astype(BF16)
-    gate = jax.nn.sigmoid(jnp.dot(own, wg_ref[...], preferred_element_type=F32))
-    keys = jnp.dot(everyone, wkv_ref[:, :width], preferred_element_type=F32).astype(BF16)
-    values = jnp.dot(everyone, wkv_ref[:, width:], preferred_element_type=F32).astype(BF16)
-    head_of = lax.broadcasted_iota(jnp.int32, (own.shape[0], width), 1) // head_dim
-    attended = jnp.zeros(own.shape, F32)
-    zero = jnp.zeros_like(queries)
-    for h in range(heads):
-        query = jnp.where(head_of == h, queries, zero)
-        scores = lax.dot_general(query, keys, dims_nt, preferred_element_type=F32)
-        scores = scores * (LOG2E / math.sqrt(head_dim)) + bias_s[h]
-        exponent = jnp.exp2(scores - jnp.max(scores, axis=-1, keepdims=True))
-        inverse = 1.0 / jnp.sum(exponent, axis=-1, keepdims=True)
-        weights = (exponent * inverse).astype(BF16)
-        summed = jnp.dot(weights, values, preferred_element_type=F32)
-        attended = jnp.where(head_of == h, summed, attended)
-    attended = (gate * attended).astype(BF16)
-    out = (msa_ref[0].astype(F32) + jnp.dot(attended, wo_ref[...], preferred_element_type=F32)).astype(BF16)
-    out_ref[0] = out
-    opm_normed = layer_normalize(out)
-    for n in range(width // 128):
-        opm_s[n] = opm_normed[:, n * 128 : n * 128 + 128]
-    left = jnp.zeros((own.shape[0] // group, 128), F32)
-    for b in range(group):
+    row_head = lax.broadcasted_iota(jnp.int32, (width, queries), 0) // head_dim
+    for i in range(seqs):
+        own = x_ref[col, i]
+        query = nt_dot(wt_s[0], own).astype(BF16)
+        for h in range(heads):
+            q_s[i, h // 2, :, (h % 2) * queries : (h % 2 + 1) * queries] = jnp.where(row_head == h, query, jnp.zeros_like(query))
+        gate_s[i] = jax.nn.sigmoid(nt_dot(wt_s[2], own))
+        for c in range(8):
+            part = x_ref[c, i]
+            k_s[i, c * 128 : c * 128 + 128] = dot(part, wkv_ref[:, :width]).astype(BF16)
+            vt_s[i, :, c * 128 : c * 128 + 128] = nt_dot(wt_s[1], part).astype(BF16)
+
+    steps = seqs * heads // 2
+    per_seq = heads // 2
+    state = {}
+
+    def score(n, k):
+        i, g = divmod(n, per_seq)
+        rows = pl.ds(k * chunk, chunk)
+        scores = dot(k_s[i, rows], q_s[i, g]) * (LOG2E / math.sqrt(head_dim)) + bias_s[g, rows]
+        t_s[n % 3, rows] = scores
+        highest = jnp.max(scores.reshape(chunk // 8, 8, both), axis=0)
+        state[n, "max"] = highest if k == 0 else jnp.maximum(state[n, "max"], highest)
+        if k == keys // chunk - 1:
+            state[n, "max"] = jnp.max(state[n, "max"], axis=0, keepdims=True)
+
+    def exponentiate(n, k):
+        rows = pl.ds(k * chunk, chunk)
+        exponent = jnp.exp2(t_s[n % 3, rows] - state[n, "max"])
+        t_s[n % 3, rows] = exponent
+        total = jnp.sum(exponent.reshape(chunk // 8, 8, both), axis=0)
+        state[n, "sum"] = total if k == 0 else state[n, "sum"] + total
+        if k == keys // chunk - 1:
+            state[n, "inverse"] = 1.0 / jnp.sum(state[n, "sum"], axis=0, keepdims=True)
+
+    def combine(n, k):
+        i, g = divmod(n, per_seq)
+        rows = pl.ds(k * chunk, chunk)
+        w_s[n % 2, rows] = (t_s[n % 3, rows] * state[n, "inverse"]).astype(BF16)
+        channels = pl.ds(g * 2 * head_dim, 2 * head_dim)
+        summed = dot(vt_s[i, channels, rows], w_s[n % 2, rows])
+        state[n, "out"] = summed if k == 0 else state[n, "out"] + summed
+        if k == keys // chunk - 1:
+            summed = state[n, "out"]
+            for e in range(2):
+                channels = pl.ds((2 * g + e) * head_dim, head_dim)
+                attended = summed[e * head_dim : (e + 1) * head_dim, e * queries : (e + 1) * queries]
+                att_s[i, channels] = (gate_s[i, channels] * attended).astype(BF16)
+
+    def finish(i):
+        out = (msa_ref[i].astype(F32) + tn_dot(att_s[i], wo_ref[...])).astype(BF16)
+        out_ref[i] = out
+        opm_normed = layer_normalize(out)
         for n in range(width // 128):
-            some = opm_s[n, pl.ds(b, own.shape[0] // group, stride=group), :].astype(BF16)
-            left += jnp.dot(some, left_w[b, n * 128 : n * 128 + 128], preferred_element_type=F32)
-    rows = left.shape[0]
-    left_s[pl.ds(step * rows, rows), :] = left
-    right_s[pl.ds(step * opm, opm), :] = lax.dot_general(
-        right_w[...], opm_normed.astype(BF16), dims_nt, preferred_element_type=F32
-    )
+            opm_s[i, n] = opm_normed[:, n * 128 : n * 128 + 128]
+        rows = queries // group
+        left = jnp.zeros((rows, 128), F32)
+        for b in range(group):
+            for n in range(width // 128):
+                some = opm_s[i, n, pl.ds(b, rows, stride=group), :].astype(BF16)
+                left += dot(some, left_w[b, n * 128 : n * 128 + 128])
+        left_s[pl.ds((step * seqs + i) * rows, rows), :] = left
+        right_s[pl.ds((step * seqs + i) * opm, opm), :] = nt_dot(wr_ref[...], opm_normed.astype(BF16))
+
+    for slot in range(steps + 2):
+        for k in range(keys // chunk):
+            if slot < steps:
+                score(slot, k)
+            if 0 <= slot - 1 < steps:
+                exponentiate(slot - 1, k)
+            if 0 <= slot - 2 < steps:
+                combine(slot - 2, k)
+        if slot >= 2 and (slot - 2) % per_seq == per_seq - 1:
+            finish((slot - 2) // per_seq)
 
     @pl.when(step == pl.num_programs(0) - 1)
     def _():
@@ -407,22 +472,25 @@
     rows, columns, _ = pair_features.shape
     heads = w_bias.shape[1]
     opm = w_left.shape[1]
+    w_bias, w_left, w_right = w_bias.T, w_left.T, w_right.T
     anywhere = pl.BlockSpec(memory_space=pl.ANY)
     whole = pl.BlockSpec(memory_space=pltpu.VMEM)
-    dma, regular = pltpu.SemaphoreType.DMA, pltpu.SemaphoreType.REGULAR
+    dma = pltpu.SemaphoreType.DMA
     x_all, bias_all = pl.pallas_call(
         prepare_kernel,
         out_shape=[
             jax.ShapeDtypeStruct((8, seqs, residues, width), BF16),
             jax.ShapeDtypeStruct((16, 8, 2, 32, 128), BF16),
         ],
-        in_specs=[whole] * 3,
+        in_specs=[anywhere, anywhere, whole],
         out_specs=[anywhere] * 2,
         scratch_shapes=[
-            pltpu.VMEM((seqs, residues, width), BF16),
+            pltpu.VMEM(alignment.shape, BF16),
+            pltpu.VMEM(pair_features.shape, BF16),
+            pltpu.VMEM(alignment.shape, BF16),
             pltpu.VMEM((heads * rows, columns), F32),
             pltpu.VMEM((16, 32, columns), BF16),
-            dma, dma((16,)), dma, dma((60,)), dma((16, 4)), dma((28,)), dma((16, 4)),
+            dma((2,)), dma, dma((16,)), dma, dma((60,)), dma((16, 4)), dma((42,)), dma((16, 6)),
         ],
         compiler_params=pltpu.CompilerParams(collective_id=0, has_side_effects=True, vmem_limit_bytes=24 * MIB),
         name="prepare",
@@ -431,32 +499,40 @@
     def fixed(array):
         return pl.BlockSpec(array.shape, lambda s: (0,) * array.ndim)
 
+    taken = 2
     alignment_out, left, right = pl.pallas_call(
         attend_kernel,
-        grid=(seqs,),
+        grid=(seqs // taken,),
         out_shape=[
             jax.ShapeDtypeStruct(alignment.shape, BF16),
             jax.ShapeDtypeStruct((32, 16, 128), BF16),
             jax.ShapeDtypeStruct((32, 16, 128), BF16),
         ],
         in_specs=[
-            pl.BlockSpec((8, 1, residues, width), lambda s: (0, s, 0, 0)),
-            pl.BlockSpec((1, residues, width), lambda s: (s, 0, 0)),
+            pl.BlockSpec((8, taken, residues, width), lambda s: (0, s, 0, 0)),
+            pl.BlockSpec((taken, residues, width), lambda s: (s, 0, 0)),
             fixed(bias_all), fixed(query_weight), fixed(key_value_weight), fixed(gate_weight), fixed(w_out), fixed(w_left),
             fixed(w_right),
         ],
         out_specs=[
-            pl.BlockSpec((1, residues, width), lambda s: (s, 0, 0)),
+            pl.BlockSpec((taken, residues, width), lambda s: (s, 0, 0)),
             pl.BlockSpec((32, 16, 128), lambda s: (0, 0, 0)),
             pl.BlockSpec((32, 16, 128), lambda s: (0, 0, 0)),
         ],
         scratch_shapes=[
-            pltpu.VMEM((heads, residues, 8 * residues), F32),
+            pltpu.VMEM((heads // 2, 8 * residues, 2 * residues), F32),
             pltpu.VMEM((128 // opm, width, 128), BF16),
-            pltpu.VMEM((opm, width), BF16),
-            pltpu.VMEM((width // 128, residues, 128), F32),
+            pltpu.VMEM((taken, width // 128, residues, 128), F32),
             pltpu.VMEM((16 * 32, 128), F32),
             pltpu.VMEM((16 * 32, 128), F32),
+            pltpu.VMEM((3, width, width), BF16),
+            pltpu.VMEM((taken, 8 * residues, width), BF16),
+            pltpu.VMEM((taken, width, 8 * residues), BF16),
+            pltpu.VMEM((taken, heads // 2, width, 2 * residues), BF16),
+            pltpu.VMEM((3, 8 * residues, 2 * residues), F32),
+            pltpu.VMEM((2, 8 * residues, 2 * residues), BF16),
+            pltpu.VMEM((taken, width, residues), BF16),
+            pltpu.VMEM((taken, width, residues), F32),
         ],
         compiler_params=pltpu.CompilerParams(vmem_limit_bytes=48 * MIB),
         name="attend",

time: 177 us -> 130 us (0.73)
  Pallas kernels: 168 us -> 122 us
  local copies, waits for them, and re-layouts: 7.9 us -> 6.09 us
    pallas_call x1, Pallas kernels: 64.7 us -> 35.1 us  [shards(): pl.pallas_call(attend_kernel, grid=(seqs // taken,), out_shape=[jax.Shape...]
    pallas_call x1, Pallas kernels: 61.7 us -> 45.5 us  [shards(): pl.pallas_call(prepare_kernel, out_shape=[jax.ShapeDtypeStruct((8, seqs,...]
    unnamed x23 -> x26, local copies, waits for them, and re-layouts: 7.9 us -> 6.09 us
where the time goes in v2:
time: 130 us; the launch traced here: 129 us
  Pallas kernels  122 us (94%)
  local copies, waits for them, and re-layouts  6.09 us (5%)
    pallas_call x1, Pallas kernels, shards(): pl.pallas_call(prepare_kernel, out_shape=[jax.ShapeDtypeStruct((8, seqs,...  45.5 us
    pallas_call x1, Pallas kernels, shards(): pl.pallas_call(attend_kernel, grid=(seqs // taken,), out_shape=[jax.Shape...  35.1 us
    pallas_call x1, Pallas kernels, shards(): pl.pallas_call(exchange_kernel, out_shape=[jax.ShapeDtypeStruct((16, 256,...  27.9 us
    pallas_call x1, Pallas kernels, shards(): pl.pallas_call(functools.partial(outer_kernel, seqs=16 * seqs), grid=(row...  13.4 us
    unnamed x26, local copies, waits for them, and re-layouts  6.09 us

profile of v2, /device:TPU:0, one launch (start us, length us, event | category | flops | bytes accessed | tf_op | source)
XLA Modules:
  0.0 128.8 jit_solution(18404947105514347735)
XLA Ops:
  0.6 0.0 copy-start
  0.6 1.6 %copy-done = bf16[64,128,128]{2,1,0:T(8,128)(2,1)S(1)} copy-done((bf16[64,128,128]{2,1,0:T(8,128)(2,1)S(1)}, bf16[64,128,128]{2,1,0:T(8,128)(2,1)}, u32[]{:S(2)}) %copy-start) | copy-done | bytes 2097176
  2.2 1.1 copy-done.3
  3.4 0.7 copy-done.12
  4.1 0.0 copy-start.9
  4.1 0.0 copy-start.10
  4.1 0.0 copy-start.11
  4.1 45.5 %prepare.1 = (bf16[8,12,128,256]{3,2,1,0:T(8,128)(2,1)S(1)}, bf16[16,8,2,32,128]{4,3,2,1,0:T(8,128)(2,1)S(1)}) custom-call(bf16[64,128,128]{2,1,0:T(8,128)(2,1)S(1)} %copy-done, bf16[12,128,256]{2,1,0:T(8,128)(2,1)S(1)} %copy-done.3, bf16[8,128]{1,0:T(8,128)(2,1)S(1)} %bitcast.5), custom_call_target="tpu_custom_call" | custom-call | tf_op jit(solution)/shard_map/prepare/pallas_call | solution.py:479
  49.6 0.0 copy-start.2
  49.6 2.6 %copy-done.2 = bf16[8,12,128,256]{3,2,1,0:T(8,128)(2,1)} copy-done((bf16[8,12,128,256]{3,2,1,0:T(8,128)(2,1)}, bf16[8,12,128,256]{3,2,1,0:T(8,128)(2,1)S(1)}, u32[]{:S(2)}) %copy-start.2) | copy-done | bytes 6291480
  52.3 0.0 copy-done.4
  52.3 0.0 copy-done.5
  52.3 0.0 copy-done.7
  52.3 0.0 copy-done.8
  52.3 0.0 copy-done.9
  52.3 0.0 copy-done.10
  52.3 0.0 copy-done.11
  52.3 0.0 copy-start.1
  52.3 0.0 copy-start.6
  52.3 35.1 %attend.1 = (bf16[12,128,256]{2,1,0:T(8,128)(2,1)}, bf16[32,16,128]{2,1,0:T(8,128)(2,1)S(1)}, bf16[32,16,128]{2,1,0:T(8,128)(2,1)S(1)}) custom-call(bf16[8,12,128,256]{3,2,1,0:T(8,128)(2,1)} %copy-done.2, bf16[12,128,256]{2,1,0:T(8,128)(2,1)S(1)} %copy-done.4, bf16[16,8,2,32,128]{4,3,2,1,0:T(8,128)(2,1)S(1)} %get-tuple-element.10.bias_ref, ...), custom_call_target="tpu_custom_call" | custom-call | tf_op jit(solution)/shard_map/attend/pallas_call | solution.py:503
  87.4 27.9 %exchange.1 = (bf16[16,256,128]{2,1,0:T(8,128)(2,1)S(1)}, bf16[32,256,128]{2,1,0:T(8,128)(2,1)S(1)}) custom-call(bf16[32,16,128]{2,1,0:T(8,128)(2,1)S(1)} %get-tuple-element.12.left_ref, bf16[32,16,128]{2,1,0:T(8,128)(2,1)S(1)} %get-tuple-element.13.right_ref), custom_call_target="tpu_custom_call" | custom-call | tf_op jit(solution)/shard_map/exchange/pallas_call | solution.py:541
  115.3 0.0 copy-done.1
  115.3 0.0 copy-done.6
  115.3 13.4 %outer.1 = bf16[64,128,128]{2,1,0:T(8,128)(2,1)} custom-call(bf16[16,256,128]{2,1,0:T(8,128)(2,1)S(1)} %get-tuple-element.14.left_ref, bf16[32,256,128]{2,1,0:T(8,128)(2,1)S(1)} %get-tuple-element.15.right_ref, bf16[64,128,128]{2,1,0:T(8,128)(2,1)S(1)} %copy-done.1, bf16[1024,128]{1,0:T(8,128)(2,1)S(1)} %copy-done.6), custom_call_target="tpu_custom_call" | custom-call | tf_op jit(solution)/shard_map/outer/pallas_call | solution.py:554
  (6 shorter events, 0.0 us)
Async XLA Ops:
  0.6 1.6 %copy-start = (bf16[64,128,128]{2,1,0:T(8,128)(2,1)S(1)}, bf16[64,128,128]{2,1,0:T(8,128)(2,1)}, u32[]{:S(2)}) copy-start(bf16[64,128,128]{2,1,0:T(8,128)(2,1)} %pair_ref.1) | copy-start | bytes 6291460
  2.2 1.1 copy-start.3
  3.4 0.7 copy-start.12
  4.0 48.2 %copy-start.4 = (bf16[12,128,256]{2,1,0:T(8,128)(2,1)S(1)}, bf16[12,128,256]{2,1,0:T(8,128)(2,1)}, u32[]{:S(2)}) copy-start(bf16[12,128,256]{2,1,0:T(8,128)(2,1)} %msa_ref.1) | copy-start | bytes 2359300
  4.0 48.2 %copy-start.5 = (bf16[256,512]{1,0:T(8,128)(2,1)S(1)}, bf16[256,512]{1,0:T(8,128)(2,1)}, u32[]{:S(2)}) copy-start(bf16[256,512]{1,0:T(8,128)(2,1)} %wkv_ref.1) | copy-start | bytes 786436
  4.0 48.2 %copy-start.7 = (bf16[256,256]{1,0:T(8,128)(2,1)S(1)}, bf16[256,256]{1,0:T(8,128)(2,1)}, u32[]{:S(2)}) copy-start(bf16[256,256]{1,0:T(8,128)(2,1)} %wq_ref.1) | copy-start | bytes 393220
  4.0 48.2 %copy-start.8 = (bf16[256,256]{1,0:T(8,128)(2,1)S(1)}, bf16[256,256]{1,0:T(8,128)(2,1)}, u32[]{:S(2)}) copy-start(bf16[256,256]{1,0:T(8,128)(2,1)} %wg_ref.1) | copy-start | bytes 393220
  4.1 48.2 %copy-start.9 = (bf16[256,256]{1,0:T(8,128)(2,1)S(1)}, bf16[256,256]{1,0:T(8,128)(2,1)}, u32[]{:S(2)}) copy-start(bf16[256,256]{1,0:T(8,128)(2,1)} %wo_ref.2) | copy-start | bytes 393220
  4.1 48.2 %copy-start.10 = (bf16[256,32]{0,1:T(8,128)(2,1)S(1)}, bf16[256,32]{0,1:T(8,128)(2,1)}, u32[]{:S(2)}) copy-start(bf16[256,32]{0,1:T(8,128)(2,1)} %param.17) | copy-start | bytes 49156
  4.1 48.2 %copy-start.11 = (bf16[256,32]{0,1:T(8,128)(2,1)S(1)}, bf16[256,32]{0,1:T(8,128)(2,1)}, u32[]{:S(2)}) copy-start(bf16[256,32]{0,1:T(8,128)(2,1)} %param.18) | copy-start | bytes 49156
  49.6 2.7 %copy-start.2 = (bf16[8,12,128,256]{3,2,1,0:T(8,128)(2,1)}, bf16[8,12,128,256]{3,2,1,0:T(8,128)(2,1)S(1)}, u32[]{:S(2)}) copy-start(bf16[8,12,128,256]{3,2,1,0:T(8,128)(2,1)S(1)} %get-tuple-element.9.x_ref) | copy-start | bytes 18874372
  52.3 63.0 %copy-start.1 = (bf16[64,128,128]{2,1,0:T(8,128)(2,1)S(1)}, bf16[64,128,128]{2,1,0:T(8,128)(2,1)}, u32[]{:S(2)}) copy-start(bf16[64,128,128]{2,1,0:T(8,128)(2,1)} %pair_ref.1) | copy-start | bytes 6291460
  52.3 63.0 %copy-start.6 = (bf16[1024,128]{1,0:T(8,128)(2,1)S(1)}, bf16[1024,128]{1,0:T(8,128)(2,1)}, u32[]{:S(2)}) copy-start(bf16[1024,128]{1,0:T(8,128)(2,1)} %wo_ref.3) | copy-start | bytes 786436

commit v3 on v2

v3 whole, which is shorter than its diff:
```python
import functools
import math

import jax
import jax.numpy as jnp
from jax import lax
from jax.experimental import pallas as pl
from jax.experimental.pallas import tpu as pltpu
from jax.sharding import PartitionSpec as P

EPS = 1e-05
LOG2E = math.log2(math.e)
MESH = pl.DeviceIdType.MESH
F32, BF16 = jnp.float32, jnp.bfloat16
MIB = 1 << 20

RINGS = ({0: (1, 3), 1: (2,)}, {0: (1, 3), 3: (2,)})


def layer_normalize(values_in):
    values_in = values_in.astype(F32)
    average = jnp.mean(values_in, axis=-1, keepdims=True)
    centered = values_in - average
    variance = jnp.mean(centered * centered, axis=-1, keepdims=True)
    return centered * lax.rsqrt(variance + EPS)


class Place:
    def __init__(self):
        self.grp, self.row, self.col = (lax.axis_index(a) for a in ("grp", "row", "col"))
        self.x = 2 * self.grp + self.row % 2
        self.z = self.row // 2
        self.y = self.col // 2
        self.core = self.col % 2
        self.plane = 8 * self.grp + self.row

    def plane_index(self, dx, dz):
        x, z = (self.x + dx + 4) % 4, (self.z + dz + 4) % 4
        return 8 * (x // 2) + 2 * z + x % 2

    def in_plane(self, dx, dz):
        index = self.plane_index(dx, dz)
        return (index // 8, index % 8, self.col)

    def col_index(self, dy, dk):
        return 2 * ((self.y + dy + 4) % 4) + (self.core + dk) % 2

    def in_col(self, dy, dk):
        return (self.grp, self.row, self.col_index(dy, dk))


def plane_events():
    events = []
    for q in range(4):
        ring = RINGS[q % 2]
        level, depth = [(0, 0)], 0
        while level:
            following = []
            for first, second in level:
                kids = [(f, second) for f in ring.get(first, ())] if second == 0 else []
                kids += [(first, s) for s in ring.get(second, ())]
                turn = (lambda n: n) if q < 2 else (lambda n: (n[1], n[0]))
                events.append((depth, q, turn((first, second)), [turn(kid) for kid in kids]))
                following += kids
            level, depth = following, depth + 1
    return events


def col_events(pieces):
    events = []
    for q in range(pieces):
        ring = RINGS[q % 2]
        level, depth = [(0, 0)], 0
        while level:
            following = []
            for dy, dk in level:
                kids = [(d, 0) for d in ring.get(dy, ())] + [(dy, 1)] if dk == 0 else []
                events.append((depth, q, (dy, dk), kids))
                following += kids
            level, depth = following, depth + 1
    return events


class Spread:
    def __init__(self, target, source_of, slot, own, send_sem, recv_sem):
        self.target, self.source_of, self.slot, self.own = target, source_of, slot, own
        self.send_sem, self.recv_sem = send_sem, recv_sem
        self.started = []

    def copy(self, node, kid, q, n):
        here = self.slot(self.source_of(-node[0], -node[1]), q)
        return pltpu.make_async_remote_copy(
            src_ref=self.own(q) if node == (0, 0) else here,
            dst_ref=here,
            send_sem=self.send_sem.at[n],
            recv_sem=self.recv_sem.at[kid[0] * 4 + kid[1], q],
            device_id=self.target((kid[0] - node[0]) % 4, (kid[1] - node[1]) % 4),
            device_id_type=MESH,
        )

    def run(self, event):
        _, q, node, kids = event
        if node != (0, 0):
            here = self.slot(self.source_of(-node[0], -node[1]), q)
            pltpu.make_async_copy(here, here, self.recv_sem.at[node[0] * 4 + node[1], q]).wait()
        for kid in kids:
            self.copy(node, kid, q, len(self.started)).start()
            self.started.append((node, kid, q, len(self.started)))

    def finish(self):
        for started in self.started:
            self.copy(*started).wait_send()


def greet(place, partners, others):
    barrier = pltpu.get_barrier_semaphore()
    for partner in partners:
        pl.semaphore_signal(barrier, inc=1, device_id=partner, device_id_type=MESH)
    for other in others:
        pl.semaphore_signal(barrier, inc=1, device_id=other, device_id_type=MESH)
    return barrier, len(partners) + len(others)


def neighbours(place):
    return [place.in_plane(1, 0), place.in_plane(3, 0), place.in_plane(0, 1), place.in_plane(0, 3),
            place.in_col(1, 0), place.in_col(3, 0), place.in_col(0, 1)]


def scatter(copies, send_sem, recv_sem):
    started = []
    for n, (source, destination, device, is_self) in enumerate(copies):
        remote = pltpu.make_async_remote_copy(
            src_ref=source, dst_ref=destination, send_sem=send_sem.at[n], recv_sem=recv_sem, device_id=device, device_id_type=MESH
        )
        if is_self is None:
            remote.start()
        else:
            pl.when(jnp.logical_not(is_self))(remote.start)
            pl.when(is_self)(pltpu.make_async_copy(source, destination, recv_sem).start)
        started.append((remote, is_self))

    def finish():
        for remote, is_self in started:
            if is_self is None:
                remote.wait_send()
            else:
                pl.when(jnp.logical_not(is_self))(remote.wait_send)

    return finish


def nt_dot(a, b):
    return lax.dot_general(a, b, (((1,), (1,)), ((), ())), preferred_element_type=F32)


def tn_dot(a, b):
    return lax.dot_general(a, b, (((0,), (0,)), ((), ())), preferred_element_type=F32)


def dot(a, b):
    return jnp.dot(a, b, preferred_element_type=F32)


def unit(rows, columns, shift=0):
    row = lax.broadcasted_iota(jnp.int32, (rows, columns), 0)
    column = lax.broadcasted_iota(jnp.int32, (rows, columns), 1)
    return (column == row + shift).astype(F32).astype(BF16)


def block_kernel(
    pair_hbm, msa_hbm, wb_ref, wq_ref, wkv_ref, wg_ref, wo_ref, wl_ref, wr_ref,
    out_ref, left_all, right_all,
    msa_ref, pair_ref, x_all, bias_all, tile32, tile,
    bias_s, left_w, opm_s, left_s, right_s, left_v, right_v, wt_s, k_s, vt_s, q_s, t_s, w_s, att_s, last_att, gate_s,
    in_sem, local_sem, scatter_send, scatter_recv, bias_send, bias_recv, x_send, x_recv,
    spread_send, spread_recv, left_send, left_recv, right_send, right_recv,
):
    get_msa = pltpu.make_async_copy(msa_hbm, msa_ref, in_sem.at[0])
    get_msa.start()
    get_pair = pltpu.make_async_copy(pair_hbm, pair_ref, in_sem.at[1])
    get_pair.start()
    place = Place()
    factor_col = place.plane // 2
    barrier, expected = greet(
        place,
        neighbours(place),
        [((2 * place.col + u) // 8, (2 * place.col + u) % 8, c) for u in range(2) for c in range(8)]
        + [(r // 8, r % 8, factor_col) for r in range(16)],
    )

    seqs, queries, width = msa_ref.shape
    taken = k_s.shape[0]
    pieces = seqs // taken
    x_spread = Spread(
        place.in_col,
        place.col_index,
        lambda source, q: x_all.at[source, pl.ds(q * taken, taken)],
        lambda q: x_all.at[place.col, pl.ds(q * taken, taken)],
        x_send,
        x_recv,
    )
    x_steps = [[[e for e in col_events(pieces) if e[1] == q and e[0] == d] for d in range(4)] for q in range(pieces)]

    def x_run(q, depth):
        for event in x_steps[q][depth]:
            x_spread.run(event)

    get_msa.wait()

    @pl.loop(0, seqs)
    def _(s):
        x_all[place.col, s] = layer_normalize(msa_ref[s]).astype(BF16)

    pl.semaphore_wait(barrier, expected)
    x_run(0, 0)

    rows = pair_ref.shape[0]
    heads = wb_ref.shape[0]
    get_pair.wait()

    def bias_of_rows(first, last):
        @pl.loop(first, last, unroll=8)
        def _(i):
            pair_normed = layer_normalize(pair_ref[i]).astype(BF16)
            tile32[pl.ds(i, heads, stride=rows), :] = nt_dot(wb_ref[...], pair_normed)

    bias_of_rows(0, rows // 2)
    x_run(0, 1)
    bias_of_rows(rows // 2, rows)
    tile[...] = tile32[...].astype(BF16).reshape(tile.shape)

    target_col = place.plane // 2
    copies = []
    for t in range(16):
        piece = (place.plane + t) % 16
        copies.append(
            (
                tile.at[piece],
                bias_all.at[piece, place.col, place.plane % 2],
                (piece // 8, piece % 8, target_col),
                target_col == place.col if t == 0 else None,
            )
        )
    scatter_finish = scatter(copies, scatter_send, scatter_recv)
    x_run(1, 0)

    opm = wl_ref.shape[0]
    group = 128 // opm
    head_dim = width // heads
    both = 2 * queries
    keys = k_s.shape[1]
    chunk = 256
    left_s[...] = jnp.zeros_like(left_s)
    right_s[...] = jnp.zeros_like(right_s)
    att_s[...] = jnp.zeros_like(att_s)
    for b in range(group):
        left_w[b] = tn_dot(wl_ref[...], unit(opm, 128, b * opm)).astype(BF16)
    wt_s[0] = wq_ref[...].T
    wt_s[1] = wkv_ref[:, width:].T
    wt_s[2] = wg_ref[...].T

    mine = bias_all.at[place.plane]
    bias_spread = Spread(
        place.in_plane,
        place.plane_index,
        lambda source, q: bias_all.at[source, pl.ds(2 * q, 2)],
        lambda q: bias_all.at[place.plane, pl.ds(2 * q, 2)],
        bias_send,
        bias_recv,
    )
    todo = []
    for depth in range(5):
        todo += [(13 + 4.2 * depth, 0, functools.partial(bias_spread.run, e)) for e in plane_events() if e[0] == depth]
    for q in range(pieces):
        direct = 6.5 if q == 0 else 14.5 + 5 * (q - 1)
        if q > 1:
            todo.append((direct - 6, 1, functools.partial(x_run, q, 0)))
        if q > 0:
            todo.append((direct, 2, functools.partial(x_run, q, 1)))
        todo.append((direct + 4.5, 3, functools.partial(x_run, q, 2)))
        todo.append((direct + 5.5, 4, functools.partial(x_run, q, 3)))
    todo.sort(key=lambda item: item[:2])
    pltpu.make_async_copy(mine, mine, scatter_recv).wait()
    enough = 13 + 4.2 * 4
    for _, _, run in [item for item in todo if item[0] <= enough]:
        run()
    during = [item for item in todo if item[0] > enough]

    turn = unit(128, 128)
    for h in range(heads):
        for c in range(8):
            block = jnp.concatenate([bias_all[2 * h + v, c, u] for u in range(2) for v in range(2)], axis=0)
            bias_s[h // 2, c * 128 : c * 128 + 128, (h % 2) * 128 : (h % 2) * 128 + 128] = nt_dot(turn, block) * LOG2E

    row_head = lax.broadcasted_iota(jnp.int32, (width, queries), 0) // head_dim
    per_seq = heads // 2
    slots = taken * per_seq

    def project(step, i):
        own = x_all[place.col, step * taken + i]
        query = nt_dot(wt_s[0], own).astype(BF16)
        for h in range(heads):
            q_s[i, h // 2, :, (h % 2) * queries : (h % 2 + 1) * queries] = jnp.where(row_head == h, query, jnp.zeros_like(query))
        gate_s[i] = jax.nn.sigmoid(nt_dot(wt_s[2], own))
        for c in range(8):
            part = x_all[c, step * taken + i]
            k_s[i, c * 128 : c * 128 + 128] = dot(part, wkv_ref[:, :width]).astype(BF16)
            vt_s[i, :, c * 128 : c * 128 + 128] = nt_dot(wt_s[1], part).astype(BF16)

    state = {}

    def score(n, k):
        i, g = divmod(n, per_seq)
        rows = pl.ds(k * chunk, chunk)
        scores = dot(k_s[i, rows], q_s[i, g]) * (LOG2E / math.sqrt(head_dim)) + bias_s[g, rows]
        t_s[n % 3, rows] = scores
        highest = jnp.max(scores.reshape(chunk // 8, 8, both), axis=0)
        state[n, "max"] = highest if k == 0 else jnp.maximum(state[n, "max"], highest)
        if k == keys // chunk - 1:
            state[n, "max"] = jnp.max(state[n, "max"], axis=0, keepdims=True)

    def exponentiate(n, k):
        rows = pl.ds(k * chunk, chunk)
        exponent = jnp.exp2(t_s[n % 3, rows] - state[n, "max"])
        t_s[n % 3, rows] = exponent
        total = jnp.sum(exponent.reshape(chunk // 8, 8, both), axis=0)
        state[n, "sum"] = total if k == 0 else state[n, "sum"] + total
        if k == keys // chunk - 1:
            state[n, "inverse"] = 1.0 / jnp.sum(state[n, "sum"], axis=0, keepdims=True)

    def combine(n, k):
        i, g = divmod(n, per_seq)
        rows = pl.ds(k * chunk, chunk)
        w_s[n % 2, rows] = (t_s[n % 3, rows] * state[n, "inverse"]).astype(BF16)
        channels = pl.ds(g * 2 * head_dim, 2 * head_dim)
        summed = dot(vt_s[i, channels, rows], w_s[n % 2, rows])
        state[n, "out"] = summed if k == 0 else state[n, "out"] + summed
        if k == keys // chunk - 1:
            summed = state[n, "out"]
            for e in range(2):
                channels = pl.ds((2 * g + e) * head_dim, head_dim)
                attended = summed[e * head_dim : (e + 1) * head_dim, e * queries : (e + 1) * queries]
                att_s[i, channels] = (gate_s[i, channels] * attended).astype(BF16)

    def finish(step, i, att, part):
        seq = step * taken + i
        if part == 0:
            out_ref[seq] = (msa_ref[seq].astype(F32) + tn_dot(att[i], wo_ref[...])).astype(BF16)
        if part == 1:
            opm_normed = layer_normalize(out_ref[seq])
            for n in range(width // 128):
                opm_s[i, n] = opm_normed[:, n * 128 : n * 128 + 128]
        rows = queries // group
        if part == 2:
            left = jnp.zeros((rows, 128), F32)
            for b in range(group):
                for n in range(width // 128):
                    some = opm_s[i, n, pl.ds(b, rows, stride=group), :].astype(BF16)
                    left += dot(some, left_w[b, n * 128 : n * 128 + 128])
            left_s[pl.ds(seq * rows, rows), :] = left
        if part == 3:
            right = jnp.zeros((opm, queries), F32)
            for n in range(width // 128):
                right += nt_dot(wr_ref[:, n * 128 : n * 128 + 128], opm_s[i, n].astype(BF16))
            right_s[pl.ds(seq * opm, opm), :] = right

    @pl.loop(0, pieces)
    def _(step):
        for n in range(1, 3):

            @pl.when(step == n)
            def _(n=n):
                for at, _, run in during:
                    if (at > 36) == (n == 2):
                        run()

        last_att[...] = att_s[...]
        before = jnp.maximum(step - 1, 0)
        for i in range(taken):
            project(step, i)
        for slot in range(slots + 2):
            for k in range(keys // chunk):
                if slot < slots:
                    score(slot, k)
                if 0 <= slot - 1 < slots:
                    exponentiate(slot - 1, k)
                if 0 <= slot - 2 < slots:
                    combine(slot - 2, k)
                if k == 0 and 1 <= slot <= 4 * taken:
                    finish(before, (slot - 1) // 4, last_att, (slot - 1) % 4)

    for part in range(4):
        for i in range(taken):
            finish(pieces - 1, i, att_s, part)
    for n in range(32):
        left_v[n] = left_s[pl.ds(n, 16, stride=32), :].astype(BF16)
        right_v[n] = right_s[pl.ds(n, 16, stride=32), :].astype(BF16)

    def rows_of(source):
        return pl.ds(pl.multiple_of(source * 16, 16), 16)

    copies = []
    for half in range(2):
        row = 2 * place.col + half
        for t in range(8):
            c = (place.col + t) % 8
            copies.append(
                (
                    left_v.at[pl.ds(16 * half + 2 * c, 2)],
                    left_all.at[pl.ds(2 * c, 2), rows_of(place.plane)],
                    (row // 8, row % 8, c),
                    row == place.plane if t == 0 else None,
                )
            )
    spread_finish = scatter(copies, spread_send, spread_recv)
    right_spread = Spread(
        place.in_plane,
        place.plane_index,
        lambda source, q: right_all.at[pl.ds(8 * q, 8), rows_of(source)],
        lambda q: right_v.at[pl.ds(8 * q, 8)],
        right_send,
        right_recv,
    )
    plane = plane_events()
    for event in [e for e in plane if e[0] == 0]:
        right_spread.run(event)
    keep = pltpu.make_async_copy(right_v, right_all.at[:, rows_of(place.plane)], local_sem)
    keep.start()
    mine = left_all.at[pl.ds(2 * place.col, 2)]
    left_spread = Spread(
        place.in_col,
        place.col_index,
        lambda source, q: left_all.at[2 * source + q],
        lambda q: left_all.at[2 * place.col + q],
        left_send,
        left_recv,
    )
    todo = [(3.0 * e[0], 0, right_spread, e) for e in plane if e[0] > 0]
    todo += [(4 + 3.0 * e[0], 1, left_spread, e) for e in col_events(2)]
    gathered = False
    for _, kind, spread, event in sorted(todo, key=lambda item: item[:2]):
        if kind == 1 and not gathered:
            pltpu.make_async_copy(mine, mine, spread_recv).wait()
            gathered = True
        spread.run(event)
    keep.wait()
    scatter_finish()
    spread_finish()
    for spread in (bias_spread, x_spread, left_spread, right_spread):
        spread.finish()


def outer_kernel(left_ref, right_ref, pair_ref, wo_ref, msa_ref, out_ref, msa_out, w32, w_t, products, *, seqs):
    msa_out[...] = msa_ref[...]
    opm = right_ref.shape[0]
    group = 128 // opm

    @pl.when(pl.program_id(0) == 0)
    def _():
        w32[...] = wo_ref[...].astype(F32)
        turned = jnp.concatenate([w32[pl.ds(d, opm, stride=opm), :] for d in range(opm)], axis=0)
        w_t[...] = turned.T.astype(BF16)

    left = left_ref[0].T
    for d in range(0, opm, 2):
        right = jnp.concatenate([right_ref[d], right_ref[d + 1]], axis=1)
        product = (jnp.dot(left, right, preferred_element_type=F32) * (1.0 / seqs)).astype(BF16)
        for b in range(group):
            for e in range(2):
                products[b // 2, (d + e) * opm : (d + e + 1) * opm, (b % 2) * 128 : (b % 2) * 128 + 128] = product[
                    b * opm : (b + 1) * opm, e * 128 : e * 128 + 128
                ]
    for pair in range(group // 2):
        update = jnp.dot(w_t[...], products[pair], preferred_element_type=F32)
        for e in range(2):
            b = 2 * pair + e
            out_ref[b] = (pair_ref[b].astype(F32) + update[:, e * 128 : e * 128 + 128].T).astype(BF16)


def shards(
    alignment, pair_features, w_bias, query_weight, key_value_weight, gate_weight, w_out, w_left, w_right, w_outer
):
    seqs, residues, width = alignment.shape
    rows, columns, _ = pair_features.shape
    heads = w_bias.shape[1]
    opm = w_left.shape[1]
    taken = 2
    keys = 8 * residues
    anywhere = pl.BlockSpec(memory_space=pl.ANY)
    whole = pl.BlockSpec(memory_space=pltpu.VMEM)
    dma = pltpu.SemaphoreType.DMA
    alignment_out, left_all, right_all = pl.pallas_call(
        block_kernel,
        out_shape=[
            jax.ShapeDtypeStruct(alignment.shape, BF16),
            jax.ShapeDtypeStruct((16, 256, 128), BF16),
            jax.ShapeDtypeStruct((32, 256, 128), BF16),
        ],
        in_specs=[anywhere] * 2 + [whole] * 7,
        out_specs=[whole, anywhere, anywhere],
        scratch_shapes=[
            pltpu.VMEM(alignment.shape, BF16),
            pltpu.VMEM(pair_features.shape, BF16),
            pltpu.VMEM((8, seqs, residues, width), BF16),
            pltpu.VMEM((16, 8, 2, 32, 128), BF16),
            pltpu.VMEM((heads * rows, columns), F32),
            pltpu.VMEM((16, 32, columns), BF16),
            pltpu.VMEM((heads // 2, keys, 2 * residues), F32),
            pltpu.VMEM((128 // opm, width, 128), BF16),
            pltpu.VMEM((taken, width // 128, residues, 128), F32),
            pltpu.VMEM((16 * 32, 128), F32),
            pltpu.VMEM((16 * 32, 128), F32),
            pltpu.VMEM((32, 16, 128), BF16),
            pltpu.VMEM((32, 16, 128), BF16),
            pltpu.VMEM((3, width, width), BF16),
            pltpu.VMEM((taken, keys, width), BF16),
            pltpu.VMEM((taken, width, keys), BF16),
            pltpu.VMEM((taken, heads // 2, width, 2 * residues), BF16),
            pltpu.VMEM((3, keys, 2 * residues), F32),
            pltpu.VMEM((2, keys, 2 * residues), BF16),
            pltpu.VMEM((taken, width, residues), BF16),
            pltpu.VMEM((taken, width, residues), BF16),
            pltpu.VMEM((taken, width, residues), F32),
            dma((2,)), dma, dma((16,)), dma, dma((60,)), dma((16, 4)), dma((42,)), dma((16, 6)),
            dma((16,)), dma, dma((14,)), dma((16, 2)), dma((60,)), dma((16, 4)),
        ],
        compiler_params=pltpu.CompilerParams(collective_id=0, has_side_effects=True, vmem_limit_bytes=56 * MIB),
        name="block",
    )(
        pair_features, alignment, w_bias.T, query_weight, key_value_weight, gate_weight, w_out, w_left.T, w_right.T
    )

    steps = rows * opm // 128
    flat = (seqs * residues, width)
    share = pl.BlockSpec((flat[0] // steps, width), lambda a: (a, 0))
    pair_out, alignment_out = pl.pallas_call(
        functools.partial(outer_kernel, seqs=16 * seqs),
        grid=(steps,),
        out_shape=[jax.ShapeDtypeStruct(pair_features.shape, BF16), jax.ShapeDtypeStruct(flat, BF16)],
        in_specs=[
            pl.BlockSpec((1, 256, 128), lambda a: (a, 0, 0)),
            pl.BlockSpec((32, 256, 128), lambda a: (0, 0, 0)),
            pl.BlockSpec((128 // opm, columns, 128), lambda a: (a, 0, 0)),
            pl.BlockSpec(w_outer.shape, lambda a: (0, 0)),
            share,
        ],
        out_specs=[pl.BlockSpec((128 // opm, columns, 128), lambda a: (a, 0, 0)), share],
        scratch_shapes=[
            pltpu.VMEM(w_outer.shape, F32),
            pltpu.VMEM(w_outer.shape[::-1], BF16),
            pltpu.VMEM((128 // opm // 2, w_outer.shape[0], 256), BF16),
        ],
        compiler_params=pltpu.CompilerParams(vmem_limit_bytes=56 * MIB),
        name="outer",
    )(left_all, right_all, pair_features, w_outer, alignment_out.reshape(flat))
    return (alignment_out.reshape(alignment.shape), pair_out)


def solution(mesh):
    rows = P(("grp", "row"), "col", None)
    in_specs = (rows, rows) + (P(),) * 8
    return jax.shard_map(shards, mesh=mesh, in_specs=in_specs, out_specs=(rows, rows), check_vma=False)
```

time: 130 us -> 119 us (0.915)
  local copies, waits for them, and re-layouts: 6.09 us -> 0 us
  Pallas kernels: 122 us -> 118 us
    unnamed x26 -> x0, local copies, waits for them, and re-layouts: 6.09 us -> none
    pallas_call x4 -> x2, Pallas kernels: 122 us -> 118 us  [the longest x1 101 us: shards(): pl.pallas_call(block_kernel, out_shape=[jax.ShapeDtypeStruct(alignment.sh...]
where the time goes in v3:
time: 119 us; the launch traced here: 118 us
  Pallas kernels  118 us (99%)
    pallas_call x1, Pallas kernels, shards(): pl.pallas_call(block_kernel, out_shape=[jax.ShapeDtypeStruct(alignment.sh...  101 us
    pallas_call x1, Pallas kernels, shards(): pl.pallas_call(functools.partial(outer_kernel, seqs=16 * seqs), grid=(ste...  16.9 us

profile of v3, /device:TPU:0, one launch (start us, length us, event | category | flops | bytes accessed | tf_op | source)
XLA Modules:
  0.0 118.4 jit_solution(8183701084330505408)
XLA Ops:
  0.6 100.9 %block.1 = (bf16[12,128,256]{2,1,0:T(8,128)(2,1)}, bf16[16,256,128]{2,1,0:T(8,128)(2,1)}, bf16[32,256,128]{2,1,0:T(8,128)(2,1)}) custom-call(bf16[64,128,128]{2,1,0:T(8,128)(2,1)} %pair_ref.1, bf16[12,128,256]{2,1,0:T(8,128)(2,1)} %msa_hbm.1, bf16[8,128]{1,0:T(8,128)(2,1)} %bitcast.8, bf16[256,256]{1,0:T(8,128)(2,1)} %wq_ref.1, bf16[256,512]{1,0:T(8,128)(2,1)} %wkv_ref.1, ...), custom_call_target="tpu_custom_call" | custom-call | tf_op jit(solution)/shard_map/block/pallas_call | solution.py:492
  101.5 16.9 %outer.1 = (bf16[64,128,128]{2,1,0:T(8,128)(2,1)}, bf16[1536,256]{1,0:T(8,128)(2,1)}) custom-call(bf16[16,256,128]{2,1,0:T(8,128)(2,1)} %get-tuple-element.7.left_ref, bf16[32,256,128]{2,1,0:T(8,128)(2,1)} %get-tuple-element.8.right_ref, bf16[64,128,128]{2,1,0:T(8,128)(2,1)} %pair_ref.1, bf16[1024,128]{1,0:T(8,128)(2,1)} %wo_ref.3, bf16[1536,256]{1,0:T(8,128)(2,1)} %bitcast.5), custom_call_target="tpu_custom_call" | custom-call | tf_op jit(solution)/shard_map/outer/pallas_call | solution.py:536

commit v4 on v3

--- a/solution.py
+++ b/solution.py
@@ -14,7 +14,8 @@
 F32, BF16 = jnp.float32, jnp.bfloat16
 MIB = 1 << 20
 
-RINGS = ({0: (1, 3), 1: (2,)}, {0: (1, 3), 3: (2,)})
+RELAY = ({0: (1, 3), 1: (2,)}, {0: (1, 3), 3: (2,)})
+DIRECT = {0: (2, 1, 3)}
 
 
 def layer_normalize(values_in):
@@ -51,25 +52,24 @@
 
 def plane_events():
     events = []
-    for q in range(4):
-        ring = RINGS[q % 2]
+    for q in range(2):
         level, depth = [(0, 0)], 0
         while level:
             following = []
             for first, second in level:
-                kids = [(f, second) for f in ring.get(first, ())] if second == 0 else []
-                kids += [(first, s) for s in ring.get(second, ())]
-                turn = (lambda n: n) if q < 2 else (lambda n: (n[1], n[0]))
+                kids = [(f, second) for f in DIRECT.get(first, ())] if second == 0 else []
+                kids += [(first, s) for s in DIRECT.get(second, ())]
+                turn = (lambda n: n) if q == 0 else (lambda n: (n[1], n[0]))
                 events.append((depth, q, turn((first, second)), [turn(kid) for kid in kids]))
                 following += kids
             level, depth = following, depth + 1
     return events
 
 
-def col_events(pieces):
+def col_events(pieces, rings):
     events = []
     for q in range(pieces):
-        ring = RINGS[q % 2]
+        ring = rings[q % 2]
         level, depth = [(0, 0)], 0
         while level:
             following = []
@@ -123,7 +123,8 @@
 
 def neighbours(place):
     return [place.in_plane(1, 0), place.in_plane(3, 0), place.in_plane(0, 1), place.in_plane(0, 3),
-            place.in_col(1, 0), place.in_col(3, 0), place.in_col(0, 1)]
+            place.in_plane(2, 0), place.in_plane(0, 2),
+            place.in_col(1, 0), place.in_col(3, 0), place.in_col(2, 0), place.in_col(0, 1)]
 
 
 def scatter(copies, send_sem, recv_sem):
@@ -171,7 +172,7 @@
     pair_hbm, msa_hbm, wb_ref, wq_ref, wkv_ref, wg_ref, wo_ref, wl_ref, wr_ref,
     out_ref, left_all, right_all,
     msa_ref, pair_ref, x_all, bias_all, tile32, tile,
-    bias_s, left_w, opm_s, left_s, right_s, left_v, right_v, wt_s, k_s, vt_s, q_s, t_s, w_s, att_s, last_att, gate_s,
+    bias_s, left_w, opm_s, left_s, right_s, left_v, right_v, wt_s, k_s, vt_s, q_s, t_s, w_s, att_s, gate_s, stat_s,
     in_sem, local_sem, scatter_send, scatter_recv, bias_send, bias_recv, x_send, x_recv,
     spread_send, spread_recv, left_send, left_recv, right_send, right_recv,
 ):
@@ -189,17 +190,17 @@
     )
 
     seqs, queries, width = msa_ref.shape
-    taken = k_s.shape[0]
-    pieces = seqs // taken
+    pieces = x_recv.shape[1]
+    x_part = seqs // pieces
     x_spread = Spread(
         place.in_col,
         place.col_index,
-        lambda source, q: x_all.at[source, pl.ds(q * taken, taken)],
-        lambda q: x_all.at[place.col, pl.ds(q * taken, taken)],
+        lambda source, q: x_all.at[source, pl.ds(q * x_part, x_part)],
+        lambda q: x_all.at[place.col, pl.ds(q * x_part, x_part)],
         x_send,
         x_recv,
     )
-    x_steps = [[[e for e in col_events(pieces) if e[1] == q and e[0] == d] for d in range(4)] for q in range(pieces)]
+    x_steps = [[[e for e in col_events(pieces, RELAY) if e[1] == q and e[0] == d] for d in range(4)] for q in range(pieces)]
 
     def x_run(q, depth):
         for event in x_steps[q][depth]:
@@ -218,15 +219,11 @@
     heads = wb_ref.shape[0]
     get_pair.wait()
 
-    def bias_of_rows(first, last):
-        @pl.loop(first, last, unroll=8)
-        def _(i):
-            pair_normed = layer_normalize(pair_ref[i]).astype(BF16)
-            tile32[pl.ds(i, heads, stride=rows), :] = nt_dot(wb_ref[...], pair_normed)
-
-    bias_of_rows(0, rows // 2)
-    x_run(0, 1)
-    bias_of_rows(rows // 2, rows)
+    @pl.loop(0, rows, unroll=8)
+    def _(i):
+        pair_normed = layer_normalize(pair_ref[i]).astype(BF16)
+        tile32[pl.ds(i, heads, stride=rows), :] = nt_dot(wb_ref[...], pair_normed)
+
     tile[...] = tile32[...].astype(BF16).reshape(tile.shape)
 
     target_col = place.plane // 2
@@ -242,7 +239,7 @@
             )
         )
     scatter_finish = scatter(copies, scatter_send, scatter_recv)
-    x_run(1, 0)
+    x_run(0, 1)
 
     opm = wl_ref.shape[0]
     group = 128 // opm
@@ -252,7 +249,7 @@
     chunk = 256
     left_s[...] = jnp.zeros_like(left_s)
     right_s[...] = jnp.zeros_like(right_s)
-    att_s[...] = jnp.zeros_like(att_s)
+    stat_s[...] = jnp.zeros_like(stat_s)
     for b in range(group):
         left_w[b] = tn_dot(wl_ref[...], unit(opm, 128, b * opm)).astype(BF16)
     wt_s[0] = wq_ref[...].T
@@ -263,57 +260,63 @@
     bias_spread = Spread(
         place.in_plane,
         place.plane_index,
-        lambda source, q: bias_all.at[source, pl.ds(2 * q, 2)],
-        lambda q: bias_all.at[place.plane, pl.ds(2 * q, 2)],
+        lambda source, q: bias_all.at[source, pl.ds(4 * q, 4)],
+        lambda q: bias_all.at[place.plane, pl.ds(4 * q, 4)],
         bias_send,
         bias_recv,
     )
-    todo = []
-    for depth in range(5):
-        todo += [(13 + 4.2 * depth, 0, functools.partial(bias_spread.run, e)) for e in plane_events() if e[0] == depth]
-    for q in range(pieces):
-        direct = 6.5 if q == 0 else 14.5 + 5 * (q - 1)
-        if q > 1:
-            todo.append((direct - 6, 1, functools.partial(x_run, q, 0)))
-        if q > 0:
-            todo.append((direct, 2, functools.partial(x_run, q, 1)))
-        todo.append((direct + 4.5, 3, functools.partial(x_run, q, 2)))
-        todo.append((direct + 5.5, 4, functools.partial(x_run, q, 3)))
-    todo.sort(key=lambda item: item[:2])
+    bias_todo = [[functools.partial(bias_spread.run, e) for e in plane_events() if e[0] == depth] for depth in range(3)]
+    x_todo = [functools.partial(x_run, *todo) for todo in ((0, 2), (0, 3), (1, 1), (3, 0), (2, 1), (4, 0), (1, 2), (1, 3))]
+    x_first = [functools.partial(x_run, q, 0) for q in (1, 2)]
+    during = {
+        (0, 4): ((3, 1), (5, 0), (2, 2), (2, 3)),
+        (0, 12): ((4, 1), (3, 2)),
+        (1, 0): ((3, 3),),
+        (1, 4): ((5, 1), (4, 2), (4, 3)),
+        (2, 0): ((5, 2), (5, 3)),
+    }
+
+    row_head = lax.broadcasted_iota(jnp.int32, (width, queries), 0) // head_dim
+    per_seq = heads // 2
+    taken = 4
+    slots = taken * per_seq
+    parts = keys // chunk
+
+    def project(seq, i, c):
+        i = i % 2
+        if c == 0:
+            own = x_all[place.col, seq]
+            query = nt_dot(wt_s[0], own).astype(BF16)
+            for h in range(heads):
+                q_s[i, h // 2, :, (h % 2) * queries : (h % 2 + 1) * queries] = jnp.where(
+                    row_head == h, query, jnp.zeros_like(query)
+                )
+            gate_s[i] = jax.nn.sigmoid(nt_dot(wt_s[2], own))
+        part = x_all[c, seq]
+        k_s[i, c * 128 : c * 128 + 128] = dot(part, wkv_ref[:, :width]).astype(BF16)
+        vt_s[i, :, c * 128 : c * 128 + 128] = nt_dot(wt_s[1], part).astype(BF16)
+
     pltpu.make_async_copy(mine, mine, scatter_recv).wait()
-    enough = 13 + 4.2 * 4
-    for _, _, run in [item for item in todo if item[0] <= enough]:
+    for run in bias_todo[0] + x_first + bias_todo[1] + x_todo[:2]:
         run()
-    during = [item for item in todo if item[0] > enough]
-
+    for c in range(8):
+        project(0, 0, c)
+    for run in x_todo[2:] + bias_todo[2]:
+        run()
     turn = unit(128, 128)
     for h in range(heads):
         for c in range(8):
             block = jnp.concatenate([bias_all[2 * h + v, c, u] for u in range(2) for v in range(2)], axis=0)
             bias_s[h // 2, c * 128 : c * 128 + 128, (h % 2) * 128 : (h % 2) * 128 + 128] = nt_dot(turn, block) * LOG2E
 
-    row_head = lax.broadcasted_iota(jnp.int32, (width, queries), 0) // head_dim
-    per_seq = heads // 2
-    slots = taken * per_seq
-
-    def project(step, i):
-        own = x_all[place.col, step * taken + i]
-        query = nt_dot(wt_s[0], own).astype(BF16)
-        for h in range(heads):
-            q_s[i, h // 2, :, (h % 2) * queries : (h % 2 + 1) * queries] = jnp.where(row_head == h, query, jnp.zeros_like(query))
-        gate_s[i] = jax.nn.sigmoid(nt_dot(wt_s[2], own))
-        for c in range(8):
-            part = x_all[c, step * taken + i]
-            k_s[i, c * 128 : c * 128 + 128] = dot(part, wkv_ref[:, :width]).astype(BF16)
-            vt_s[i, :, c * 128 : c * 128 + 128] = nt_dot(wt_s[1], part).astype(BF16)
 
     state = {}
 
     def score(n, k):
         i, g = divmod(n, per_seq)
         rows = pl.ds(k * chunk, chunk)
-        scores = dot(k_s[i, rows], q_s[i, g]) * (LOG2E / math.sqrt(head_dim)) + bias_s[g, rows]
-        t_s[n % 3, rows] = scores
+        scores = dot(k_s[i % 2, rows], q_s[i % 2, g]) * (LOG2E / math.sqrt(head_dim)) + bias_s[g, rows]
+        t_s[n % 4, rows] = scores
         highest = jnp.max(scores.reshape(chunk // 8, 8, both), axis=0)
         state[n, "max"] = highest if k == 0 else jnp.maximum(state[n, "max"], highest)
         if k == keys // chunk - 1:
@@ -321,8 +324,8 @@
 
     def exponentiate(n, k):
         rows = pl.ds(k * chunk, chunk)
-        exponent = jnp.exp2(t_s[n % 3, rows] - state[n, "max"])
-        t_s[n % 3, rows] = exponent
+        exponent = jnp.exp2(t_s[n % 4, rows] - state[n, "max"])
+        t_s[n % 4, rows] = exponent
         total = jnp.sum(exponent.reshape(chunk // 8, 8, both), axis=0)
         state[n, "sum"] = total if k == 0 else state[n, "sum"] + total
         if k == keys // chunk - 1:
@@ -331,21 +334,21 @@
     def combine(n, k):
         i, g = divmod(n, per_seq)
         rows = pl.ds(k * chunk, chunk)
-        w_s[n % 2, rows] = (t_s[n % 3, rows] * state[n, "inverse"]).astype(BF16)
+        w_s[n % 2, rows] = (t_s[n % 4, rows] * state[n, "inverse"]).astype(BF16)
         channels = pl.ds(g * 2 * head_dim, 2 * head_dim)
-        summed = dot(vt_s[i, channels, rows], w_s[n % 2, rows])
+        summed = dot(vt_s[i % 2, channels, rows], w_s[n % 2, rows])
         state[n, "out"] = summed if k == 0 else state[n, "out"] + summed
         if k == keys // chunk - 1:
             summed = state[n, "out"]
             for e in range(2):
                 channels = pl.ds((2 * g + e) * head_dim, head_dim)
                 attended = summed[e * head_dim : (e + 1) * head_dim, e * queries : (e + 1) * queries]
-                att_s[i, channels] = (gate_s[i, channels] * attended).astype(BF16)
-
-    def finish(step, i, att, part):
-        seq = step * taken + i
+                att_s[i % 2, channels] = (gate_s[i % 2, channels] * attended).astype(BF16)
+
+    def finish(seq, i, part):
+        i = i % 2
         if part == 0:
-            out_ref[seq] = (msa_ref[seq].astype(F32) + tn_dot(att[i], wo_ref[...])).astype(BF16)
+            out_ref[seq] = (msa_ref[seq].astype(F32) + tn_dot(att_s[i], wo_ref[...])).astype(BF16)
         if part == 1:
             opm_normed = layer_normalize(out_ref[seq])
             for n in range(width // 128):
@@ -364,34 +367,41 @@
                 right += nt_dot(wr_ref[:, n * 128 : n * 128 + 128], opm_s[i, n].astype(BF16))
             right_s[pl.ds(seq * opm, opm), :] = right
 
-    @pl.loop(0, pieces)
+    @pl.loop(0, seqs // taken)
     def _(step):
-        for n in range(1, 3):
-
-            @pl.when(step == n)
-            def _(n=n):
-                for at, _, run in during:
-                    if (at > 36) == (n == 2):
-                        run()
-
-        last_att[...] = att_s[...]
-        before = jnp.maximum(step - 1, 0)
-        for i in range(taken):
-            project(step, i)
-        for slot in range(slots + 2):
-            for k in range(keys // chunk):
-                if slot < slots:
-                    score(slot, k)
-                if 0 <= slot - 1 < slots:
-                    exponentiate(slot - 1, k)
-                if 0 <= slot - 2 < slots:
-                    combine(slot - 2, k)
-                if k == 0 and 1 <= slot <= 4 * taken:
-                    finish(before, (slot - 1) // 4, last_att, (slot - 1) % 4)
-
+        first = step * taken
+        state[slots - 1, "max"] = stat_s[0, :1]
+        state[slots - 2, "inverse"] = stat_s[1, :1]
+        for slot in range(slots):
+            for (n, at), runs in during.items():
+                if at == slot:
+
+                    @pl.when(step == n)
+                    def _(runs=runs):
+                        for q, depth in runs:
+                            x_run(q, depth)
+
+            i, turn_of = divmod(slot, per_seq)
+            for k in range(parts):
+                score(slot, k)
+                exponentiate((slot - 1) % slots, k)
+                combine((slot - 2) % slots, k)
+                if turn_of >= 2:
+                    project(jnp.minimum(first + i + 1, seqs - 1), i + 1, (turn_of - 2) * parts + k)
+                    if k % 2 == 0:
+                        finish(jnp.maximum(first + i - 1, 0), i - 1, (turn_of - 2) * 2 + k // 2)
+        stat_s[0] = jnp.broadcast_to(state[slots - 1, "max"], stat_s.shape[1:])
+        stat_s[1] = jnp.broadcast_to(state[slots - 2, "inverse"], stat_s.shape[1:])
+
+    state[slots - 1, "max"] = stat_s[0, :1]
+    state[slots - 2, "inverse"] = stat_s[1, :1]
+    for k in range(parts):
+        exponentiate(slots - 1, k)
+        combine(slots - 2, k)
+    for k in range(parts):
+        combine(slots - 1, k)
     for part in range(4):
-        for i in range(taken):
-            finish(pieces - 1, i, att_s, part)
+        finish(seqs - 1, taken - 1, part)
     for n in range(32):
         left_v[n] = left_s[pl.ds(n, 16, stride=32), :].astype(BF16)
         right_v[n] = right_s[pl.ds(n, 16, stride=32), :].astype(BF16)
@@ -416,8 +426,8 @@
     right_spread = Spread(
         place.in_plane,
         place.plane_index,
-        lambda source, q: right_all.at[pl.ds(8 * q, 8), rows_of(source)],
-        lambda q: right_v.at[pl.ds(8 * q, 8)],
+        lambda source, q: right_all.at[pl.ds(16 * q, 16), rows_of(source)],
+        lambda q: right_v.at[pl.ds(16 * q, 16)],
         right_send,
         right_recv,
     )
@@ -435,8 +445,8 @@
         left_send,
         left_recv,
     )
-    todo = [(3.0 * e[0], 0, right_spread, e) for e in plane if e[0] > 0]
-    todo += [(4 + 3.0 * e[0], 1, left_spread, e) for e in col_events(2)]
+    todo = [((5 if sum(e[2]) != 2 else 7) if e[0] == 1 else 16, 0, right_spread, e) for e in plane if e[0] > 0]
+    todo += [(6 + 3.0 * e[0], 1, left_spread, e) for e in col_events(2, (DIRECT, DIRECT))]
     gathered = False
     for _, kind, spread, event in sorted(todo, key=lambda item: item[:2]):
         if kind == 1 and not gathered:
@@ -454,6 +464,7 @@
     msa_out[...] = msa_ref[...]
     opm = right_ref.shape[0]
     group = 128 // opm
+    taken = left_ref.shape[0]
 
     @pl.when(pl.program_id(0) == 0)
     def _():
@@ -461,20 +472,29 @@
         turned = jnp.concatenate([w32[pl.ds(d, opm, stride=opm), :] for d in range(opm)], axis=0)
         w_t[...] = turned.T.astype(BF16)
 
-    left = left_ref[0].T
-    for d in range(0, opm, 2):
-        right = jnp.concatenate([right_ref[d], right_ref[d + 1]], axis=1)
-        product = (jnp.dot(left, right, preferred_element_type=F32) * (1.0 / seqs)).astype(BF16)
-        for b in range(group):
+    def multiply(a):
+        left = left_ref[a].T
+        for d in range(0, opm, 2):
+            right = jnp.concatenate([right_ref[d], right_ref[d + 1]], axis=1)
+            product = (dot(left, right) * (1.0 / seqs)).astype(BF16)
+            for b in range(group):
+                for e in range(2):
+                    products[a % 2, b // 2, (d + e) * opm : (d + e + 1) * opm, (b % 2) * 128 : (b % 2) * 128 + 128] = product[
+                        b * opm : (b + 1) * opm, e * 128 : e * 128 + 128
+                    ]
+
+    def project(a):
+        for half in range(group // 2):
+            update = dot(w_t[...], products[a % 2, half])
             for e in range(2):
-                products[b // 2, (d + e) * opm : (d + e + 1) * opm, (b % 2) * 128 : (b % 2) * 128 + 128] = product[
-                    b * opm : (b + 1) * opm, e * 128 : e * 128 + 128
-                ]
-    for pair in range(group // 2):
-        update = jnp.dot(w_t[...], products[pair], preferred_element_type=F32)
-        for e in range(2):
-            b = 2 * pair + e
-            out_ref[b] = (pair_ref[b].astype(F32) + update[:, e * 128 : e * 128 + 128].T).astype(BF16)
+                row = a * group + 2 * half + e
+                out_ref[row] = (pair_ref[row].astype(F32) + update[:, e * 128 : e * 128 + 128].T).astype(BF16)
+
+    for a in range(taken + 1):
+        if a < taken:
+            multiply(a)
+        if a > 0:
+            project(a - 1)
 
 
 def shards(
@@ -484,7 +504,6 @@
     rows, columns, _ = pair_features.shape
     heads = w_bias.shape[1]
     opm = w_left.shape[1]
-    taken = 2
     keys = 8 * residues
     anywhere = pl.BlockSpec(memory_space=pl.ANY)
     whole = pl.BlockSpec(memory_space=pltpu.VMEM)
@@ -507,22 +526,22 @@
             pltpu.VMEM((16, 32, columns), BF16),
             pltpu.VMEM((heads // 2, keys, 2 * residues), F32),
             pltpu.VMEM((128 // opm, width, 128), BF16),
-            pltpu.VMEM((taken, width // 128, residues, 128), F32),
+            pltpu.VMEM((2, width // 128, residues, 128), F32),
             pltpu.VMEM((16 * 32, 128), F32),
             pltpu.VMEM((16 * 32, 128), F32),
             pltpu.VMEM((32, 16, 128), BF16),
             pltpu.VMEM((32, 16, 128), BF16),
             pltpu.VMEM((3, width, width), BF16),
-            pltpu.VMEM((taken, keys, width), BF16),
-            pltpu.VMEM((taken, width, keys), BF16),
-            pltpu.VMEM((taken, heads // 2, width, 2 * residues), BF16),
-            pltpu.VMEM((3, keys, 2 * residues), F32),
+            pltpu.VMEM((2, keys, width), BF16),
+            pltpu.VMEM((2, width, keys), BF16),
+            pltpu.VMEM((2, heads // 2, width, 2 * residues), BF16),
+            pltpu.VMEM((4, keys, 2 * residues), F32),
             pltpu.VMEM((2, keys, 2 * residues), BF16),
-            pltpu.VMEM((taken, width, residues), BF16),
-            pltpu.VMEM((taken, width, residues), BF16),
-            pltpu.VMEM((taken, width, residues), F32),
-            dma((2,)), dma, dma((16,)), dma, dma((60,)), dma((16, 4)), dma((42,)), dma((16, 6)),
-            dma((16,)), dma, dma((14,)), dma((16, 2)), dma((60,)), dma((16, 4)),
+            pltpu.VMEM((2, width, residues), BF16),
+            pltpu.VMEM((2, width, residues), F32),
+            pltpu.VMEM((2, 8, 2 * residues), F32),
+            dma((2,)), dma, dma((16,)), dma, dma((30,)), dma((16, 2)), dma((42,)), dma((16, 6)),
+            dma((16,)), dma, dma((14,)), dma((16, 2)), dma((30,)), dma((16, 2)),
         ],
         compiler_params=pltpu.CompilerParams(collective_id=0, has_side_effects=True, vmem_limit_bytes=56 * MIB),
         name="block",
@@ -530,7 +549,8 @@
         pair_features, alignment, w_bias.T, query_weight, key_value_weight, gate_weight, w_out, w_left.T, w_right.T
     )
 
-    steps = rows * opm // 128
+    taken = 4
+    steps = rows * opm // 128 // taken
     flat = (seqs * residues, width)
     share = pl.BlockSpec((flat[0] // steps, width), lambda a: (a, 0))
     pair_out, alignment_out = pl.pallas_call(
@@ -538,17 +558,17 @@
         grid=(steps,),
         out_shape=[jax.ShapeDtypeStruct(pair_features.shape, BF16), jax.ShapeDtypeStruct(flat, BF16)],
         in_specs=[
-            pl.BlockSpec((1, 256, 128), lambda a: (a, 0, 0)),
+            pl.BlockSpec((taken, 256, 128), lambda a: (a, 0, 0)),
             pl.BlockSpec((32, 256, 128), lambda a: (0, 0, 0)),
-            pl.BlockSpec((128 // opm, columns, 128), lambda a: (a, 0, 0)),
+            pl.BlockSpec((taken * 128 // opm, columns, 128), lambda a: (a, 0, 0)),
             pl.BlockSpec(w_outer.shape, lambda a: (0, 0)),
             share,
         ],
-        out_specs=[pl.BlockSpec((128 // opm, columns, 128), lambda a: (a, 0, 0)), share],
+        out_specs=[pl.BlockSpec((taken * 128 // opm, columns, 128), lambda a: (a, 0, 0)), share],
         scratch_shapes=[
             pltpu.VMEM(w_outer.shape, F32),
             pltpu.VMEM(w_outer.shape[::-1], BF16),
-            pltpu.VMEM((128 // opm // 2, w_outer.shape[0], 256), BF16),
+            pltpu.VMEM((2, 128 // opm // 2, w_outer.shape[0], 256), BF16),
         ],
         compiler_params=pltpu.CompilerParams(vmem_limit_bytes=56 * MIB),
         name="outer",

time: 119 us -> 110 us (0.924)
  Pallas kernels: 118 us -> 109 us
    pallas_call x1, Pallas kernels: 16.9 us -> 11.8 us  [shards(): pl.pallas_call(functools.partial(outer_kernel, seqs=16 * seqs), grid=(ste...]
    pallas_call x1, Pallas kernels: 101 us -> 97 us  [shards(): pl.pallas_call(block_kernel, out_shape=[jax.ShapeDtypeStruct(alignment.sh...]
where the time goes in v4:
time: 110 us; the launch traced here: 109 us
  Pallas kernels  109 us (99%)
    pallas_call x1, Pallas kernels, shards(): pl.pallas_call(block_kernel, out_shape=[jax.ShapeDtypeStruct(alignment.sh...  97 us
    pallas_call x1, Pallas kernels, shards(): pl.pallas_call(functools.partial(outer_kernel, seqs=16 * seqs), grid=(ste...  11.8 us

profile of v4, /device:TPU:0, one launch (start us, length us, event | category | flops | bytes accessed | tf_op | source)
XLA Modules:
  0.0 109.4 jit_solution(854477378405770764)
XLA Ops:
  0.6 97.0 %block.1 = (bf16[12,128,256]{2,1,0:T(8,128)(2,1)}, bf16[16,256,128]{2,1,0:T(8,128)(2,1)}, bf16[32,256,128]{2,1,0:T(8,128)(2,1)}) custom-call(bf16[64,128,128]{2,1,0:T(8,128)(2,1)} %pair_ref.1, bf16[12,128,256]{2,1,0:T(8,128)(2,1)} %msa_hbm.1, bf16[8,128]{1,0:T(8,128)(2,1)} %bitcast.8, bf16[256,256]{1,0:T(8,128)(2,1)} %wq_ref.1, bf16[256,512]{1,0:T(8,128)(2,1)} %wkv_ref.1, ...), custom_call_target="tpu_custom_call" | custom-call | tf_op jit(solution)/shard_map/block/pallas_call | solution.py:511
  97.6 11.8 %outer.1 = (bf16[64,128,128]{2,1,0:T(8,128)(2,1)}, bf16[1536,256]{1,0:T(8,128)(2,1)}) custom-call(bf16[16,256,128]{2,1,0:T(8,128)(2,1)} %get-tuple-element.7.left_ref, bf16[32,256,128]{2,1,0:T(8,128)(2,1)} %get-tuple-element.8.right_ref, bf16[64,128,128]{2,1,0:T(8,128)(2,1)} %pair_ref.1, bf16[1024,128]{1,0:T(8,128)(2,1)} %wo_ref.3, bf16[1536,256]{1,0:T(8,128)(2,1)} %bitcast.5), custom_call_target="tpu_custom_call" | custom-call | tf_op jit(solution)/shard_map/outer/pallas_call | solution.py:556

commit v5 on v4

--- a/solution.py
+++ b/solution.py
@@ -169,9 +169,9 @@
 
 
 def block_kernel(
-    pair_hbm, msa_hbm, wb_ref, wq_ref, wkv_ref, wg_ref, wo_ref, wl_ref, wr_ref,
-    out_ref, left_all, right_all,
-    msa_ref, pair_ref, x_all, bias_all, tile32, tile,
+    pair_hbm, msa_hbm, wb_ref, wq_ref, wkv_ref, wg_ref, wo_ref, wl_ref, wr_ref, outer_ref,
+    out_ref, outer_t, left_all, right_all,
+    outer_s, msa_ref, pair_ref, x_all, bias_all, tile32, tile,
     bias_s, left_w, opm_s, left_s, right_s, left_v, right_v, wt_s, k_s, vt_s, q_s, t_s, w_s, att_s, gate_s, stat_s,
     in_sem, local_sem, scatter_send, scatter_recv, bias_send, bias_recv, x_send, x_recv,
     spread_send, spread_recv, left_send, left_recv, right_send, right_recv,
@@ -212,9 +212,6 @@
     def _(s):
         x_all[place.col, s] = layer_normalize(msa_ref[s]).astype(BF16)
 
-    pl.semaphore_wait(barrier, expected)
-    x_run(0, 0)
-
     rows = pair_ref.shape[0]
     heads = wb_ref.shape[0]
     get_pair.wait()
@@ -226,6 +223,7 @@
 
     tile[...] = tile32[...].astype(BF16).reshape(tile.shape)
 
+    pl.semaphore_wait(barrier, expected)
     target_col = place.plane // 2
     copies = []
     for t in range(16):
@@ -239,7 +237,7 @@
             )
         )
     scatter_finish = scatter(copies, scatter_send, scatter_recv)
-    x_run(0, 1)
+    x_run(0, 0)
 
     opm = wl_ref.shape[0]
     group = 128 // opm
@@ -247,15 +245,6 @@
     both = 2 * queries
     keys = k_s.shape[1]
     chunk = 256
-    left_s[...] = jnp.zeros_like(left_s)
-    right_s[...] = jnp.zeros_like(right_s)
-    stat_s[...] = jnp.zeros_like(stat_s)
-    for b in range(group):
-        left_w[b] = tn_dot(wl_ref[...], unit(opm, 128, b * opm)).astype(BF16)
-    wt_s[0] = wq_ref[...].T
-    wt_s[1] = wkv_ref[:, width:].T
-    wt_s[2] = wg_ref[...].T
-
     mine = bias_all.at[place.plane]
     bias_spread = Spread(
         place.in_plane,
@@ -297,7 +286,22 @@
         vt_s[i, :, c * 128 : c * 128 + 128] = nt_dot(wt_s[1], part).astype(BF16)
 
     pltpu.make_async_copy(mine, mine, scatter_recv).wait()
-    for run in bias_todo[0] + x_first + bias_todo[1] + x_todo[:2]:
+    for run in bias_todo[0] + x_first[:1] + [functools.partial(x_run, 0, 1)] + x_first[1:]:
+        run()
+    left_s[...] = jnp.zeros_like(left_s)
+    right_s[...] = jnp.zeros_like(right_s)
+    stat_s[...] = jnp.zeros_like(stat_s)
+    for b in range(group):
+        left_w[b] = tn_dot(wl_ref[...], unit(opm, 128, b * opm)).astype(BF16)
+    wt_s[0] = wq_ref[...].T
+    wt_s[1] = wkv_ref[:, width:].T
+    wt_s[2] = wg_ref[...].T
+    outer_s[...] = outer_ref[...].astype(F32)
+    for d in range(0, opm, 4):
+        some = jnp.concatenate([outer_s[pl.ds(d + n, opm, stride=opm), :] for n in range(4)], axis=0)
+        outer_t[:, d * opm : (d + 4) * opm] = some.T.astype(BF16)
+
+    for run in bias_todo[1] + x_todo[:2]:
         run()
     for c in range(8):
         project(0, 0, c)
@@ -400,11 +404,10 @@
         combine(slots - 2, k)
     for k in range(parts):
         combine(slots - 1, k)
-    for part in range(4):
+    for part in (0, 1, 2):
         finish(seqs - 1, taken - 1, part)
     for n in range(32):
         left_v[n] = left_s[pl.ds(n, 16, stride=32), :].astype(BF16)
-        right_v[n] = right_s[pl.ds(n, 16, stride=32), :].astype(BF16)
 
     def rows_of(source):
         return pl.ds(pl.multiple_of(source * 16, 16), 16)
@@ -423,6 +426,9 @@
                 )
             )
     spread_finish = scatter(copies, spread_send, spread_recv)
+    finish(seqs - 1, taken - 1, 3)
+    for n in range(32):
+        right_v[n] = right_s[pl.ds(n, 16, stride=32), :].astype(BF16)
     right_spread = Spread(
         place.in_plane,
         place.plane_index,
@@ -446,7 +452,7 @@
         left_recv,
     )
     todo = [((5 if sum(e[2]) != 2 else 7) if e[0] == 1 else 16, 0, right_spread, e) for e in plane if e[0] > 0]
-    todo += [(6 + 3.0 * e[0], 1, left_spread, e) for e in col_events(2, (DIRECT, DIRECT))]
+    todo += [(8 + 3.0 * e[0], 1, left_spread, e) for e in col_events(2, (DIRECT, DIRECT))]
     gathered = False
     for _, kind, spread, event in sorted(todo, key=lambda item: item[:2]):
         if kind == 1 and not gathered:
@@ -460,17 +466,11 @@
         spread.finish()
 
 
-def outer_kernel(left_ref, right_ref, pair_ref, wo_ref, msa_ref, out_ref, msa_out, w32, w_t, products, *, seqs):
+def outer_kernel(left_ref, right_ref, pair_ref, w_t, msa_ref, out_ref, msa_out, products, *, seqs):
     msa_out[...] = msa_ref[...]
     opm = right_ref.shape[0]
     group = 128 // opm
     taken = left_ref.shape[0]
-
-    @pl.when(pl.program_id(0) == 0)
-    def _():
-        w32[...] = wo_ref[...].astype(F32)
-        turned = jnp.concatenate([w32[pl.ds(d, opm, stride=opm), :] for d in range(opm)], axis=0)
-        w_t[...] = turned.T.astype(BF16)
 
     def multiply(a):
         left = left_ref[a].T
@@ -508,16 +508,18 @@
     anywhere = pl.BlockSpec(memory_space=pl.ANY)
     whole = pl.BlockSpec(memory_space=pltpu.VMEM)
     dma = pltpu.SemaphoreType.DMA
-    alignment_out, left_all, right_all = pl.pallas_call(
+    alignment_out, outer_t, left_all, right_all = pl.pallas_call(
         block_kernel,
         out_shape=[
             jax.ShapeDtypeStruct(alignment.shape, BF16),
+            jax.ShapeDtypeStruct(w_outer.shape[::-1], BF16),
             jax.ShapeDtypeStruct((16, 256, 128), BF16),
             jax.ShapeDtypeStruct((32, 256, 128), BF16),
         ],
-        in_specs=[anywhere] * 2 + [whole] * 7,
-        out_specs=[whole, anywhere, anywhere],
+        in_specs=[anywhere] * 2 + [whole] * 8,
+        out_specs=[whole, whole, anywhere, anywhere],
         scratch_shapes=[
+            pltpu.VMEM(w_outer.shape, F32),
             pltpu.VMEM(alignment.shape, BF16),
             pltpu.VMEM(pair_features.shape, BF16),
             pltpu.VMEM((8, seqs, residues, width), BF16),
@@ -546,7 +548,7 @@
         compiler_params=pltpu.CompilerParams(collective_id=0, has_side_effects=True, vmem_limit_bytes=56 * MIB),
         name="block",
     )(
-        pair_features, alignment, w_bias.T, query_weight, key_value_weight, gate_weight, w_out, w_left.T, w_right.T
+        pair_features, alignment, w_bias.T, query_weight, key_value_weight, gate_weight, w_out, w_left.T, w_right.T, w_outer
     )
 
     taken = 4
@@ -561,18 +563,16 @@
             pl.BlockSpec((taken, 256, 128), lambda a: (a, 0, 0)),
             pl.BlockSpec((32, 256, 128), lambda a: (0, 0, 0)),
             pl.BlockSpec((taken * 128 // opm, columns, 128), lambda a: (a, 0, 0)),
-            pl.BlockSpec(w_outer.shape, lambda a: (0, 0)),
+            pl.BlockSpec(outer_t.shape, lambda a: (0, 0)),
             share,
         ],
         out_specs=[pl.BlockSpec((taken * 128 // opm, columns, 128), lambda a: (a, 0, 0)), share],
         scratch_shapes=[
-            pltpu.VMEM(w_outer.shape, F32),
-            pltpu.VMEM(w_outer.shape[::-1], BF16),
             pltpu.VMEM((2, 128 // opm // 2, w_outer.shape[0], 256), BF16),
         ],
         compiler_params=pltpu.CompilerParams(vmem_limit_bytes=56 * MIB),
         name="outer",
-    )(left_all, right_all, pair_features, w_outer, alignment_out.reshape(flat))
+    )(left_all, right_all, pair_features, outer_t, alignment_out.reshape(flat))
     return (alignment_out.reshape(alignment.shape), pair_out)
 
 

time: 110 us -> 109 us (level)
  no operation moved by 1% of the time
where the time goes in v5:
time: 109 us; the launch traced here: 108 us
  Pallas kernels  108 us (99%)
    pallas_call x1, Pallas kernels, shards(): pl.pallas_call(block_kernel, out_shape=[jax.ShapeDtypeStruct(alignment.sh...  96.5 us
    pallas_call x1, Pallas kernels, shards(): pl.pallas_call(functools.partial(outer_kernel, seqs=16 * seqs), grid=(ste...  11.2 us

profile of v5, /device:TPU:0, one launch (start us, length us, event | category | flops | bytes accessed | tf_op | source)
XLA Modules:
  0.0 108.3 jit_solution(4678521387599450728)
XLA Ops:
  0.6 96.5 %block.1 = (bf16[12,128,256]{2,1,0:T(8,128)(2,1)}, bf16[128,1024]{1,0:T(8,128)(2,1)}, bf16[16,256,128]{2,1,0:T(8,128)(2,1)}, bf16[32,256,128]{2,1,0:T(8,128)(2,1)}) custom-call(bf16[64,128,128]{2,1,0:T(8,128)(2,1)} %pair_ref.1, bf16[12,128,256]{2,1,0:T(8,128)(2,1)} %msa_hbm.1, bf16[8,128]{1,0:T(8,128)(2,1)} %bitcast.8, bf16[256,256]{1,0:T(8,128)(2,1)} %wq_ref.1, ...), custom_call_target="tpu_custom_call" | custom-call | tf_op jit(solution)/shard_map/block/pallas_call | solution.py:511
  97.2 11.2 %outer.1 = (bf16[64,128,128]{2,1,0:T(8,128)(2,1)}, bf16[1536,256]{1,0:T(8,128)(2,1)}) custom-call(bf16[16,256,128]{2,1,0:T(8,128)(2,1)} %get-tuple-element.8.left_ref, bf16[32,256,128]{2,1,0:T(8,128)(2,1)} %get-tuple-element.9.right_ref, bf16[64,128,128]{2,1,0:T(8,128)(2,1)} %pair_ref.1, bf16[128,1024]{1,0:T(8,128)(2,1)} %get-tuple-element.10.w_t, ...), custom_call_target="tpu_custom_call" | custom-call | tf_op jit(solution)/shard_map/outer/pallas_call | solution.py:558
